TPU v7x, 32 devices: a whole 2x2x4 slice. The times are simulated.
32 devices in a mesh: cand: 2 (over y), gx: 4 (over z), gy: 2 (over x), wa: 2 (over core).
Axes of the slice: x: 2, y: 2, z: 4, core: 2. Of those that a mesh axis runs over, the one named last changes fastest.
Arguments:
- field: bfloat16 [4, 4, 2, 4, 4, 128, 128], P('wa', 'cand', None, 'gx', None, 'gy'), parts along dimension 1, may hold values from -6 to 6
- active_rows: int32 [4, 4], P('gx'), may hold values from 0 to 128, as said below
- kern: bfloat16 [4, 2, 4, 64, 128], P('wa'), may hold values from -0.25 to 0.25
- target: float32 [4, 64, 64], P('wa'), may hold values from 0 to 3
Outputs:
- design_grad: float32 [4, 8, 128, 128], P('gx', 'cand', 'gy'), parts along dimension 1
- intensity: float32 [4, 128, 64], P('wa', 'cand'), parts along dimension 1
There are 2 independent parts, one for each index of `cand`. A program takes and returns all parts, laid end to end along the dimension named above; an argument that names none is the same for every part. Nothing has to cross between parts.
Inputs may be any that keep to these rules, and one draw needn't show every extreme that they name: `active_rows`: live rows are counted from a tile's first cell row; tiles near the aperture's centre are full and its corners empty.
All inputs are finite; a program needn't handle non-finite values.
Results may differ from a plain program's by a relative error of at most 0.0075.
Values may be sent and summed in bfloat16 or wider, within the bound.
No kernel may reach another device: no remote copies, remote signals or barrier semaphores. Data moves between devices by JAX's collectives and lax.ppermute only.
A program may use at most 128 MiB of HBM per device.

v0:
```python
import functools

import jax
import jax.numpy as jnp
from jax import lax
from jax.experimental import pallas as pl
from jax.experimental.pallas import tpu as pltpu
from jax.sharding import PartitionSpec as P

VMEM = 16 * 2**20


def two_terms(value):
    high = value.astype(jnp.bfloat16)
    return high, (value - high.astype(jnp.float32)).astype(jnp.bfloat16)


def dot(first, second, over):
    return lax.dot_general(
        first, second, ((over[:1], over[1:]), ((), ())), preferred_element_type=jnp.float32
    )


def tile_kern(kern, wave, tile):
    real, imag = kern[wave, 0, tile], kern[wave, 1, tile]
    return jnp.concatenate([real, imag], axis=0), jnp.concatenate([-imag, real], axis=0)


def one_block(value, block, blocks):
    width = value.shape[1] // blocks
    picked = value[:, :width]
    for index in range(1, blocks):
        picked = jnp.where(block == index, value[:, index * width : (index + 1) * width], picked)
    return picked


def turn(value):
    width = value.shape[1]
    row = lax.broadcasted_iota(jnp.int32, (width, width), 0)
    column = lax.broadcasted_iota(jnp.int32, (width, width), 1)
    unit = jnp.where(row == column, 1.0, 0.0).astype(value.dtype)
    return dot(unit, value, (1, 1)).astype(value.dtype)


def twice(value, axis):
    return jnp.concatenate([value, value], axis=axis)


def diagonal(value, count):
    zero = jnp.zeros_like(value)
    rows = [
        jnp.concatenate([value if index == other else zero for other in range(count)], axis=1)
        for index in range(count)
    ]
    return jnp.concatenate(rows, axis=0)


def over_tiles(tiles, body, init):
    return lax.fori_loop(0, tiles, body, init, unroll=tiles <= 8)


def live_rows(count, shape):
    height = shape[-2]
    row = lax.axis_index("gy") * height + lax.broadcasted_iota(jnp.int32, shape, len(shape) - 2)
    return row < count


def share_kernel(rows_far, field_far, kern_far, share, field, kern, counts, rows, arrived):
    waves, polars, _, tiles, height, side = field.shape
    focus = kern.shape[3]
    copies = [pltpu.make_async_copy(rows_far, rows, arrived.at[2 * waves])]
    for wave in range(waves):
        copies += [
            pltpu.make_async_copy(kern_far.at[wave], kern.at[wave], arrived.at[2 * wave]),
            pltpu.make_async_copy(
                field_far.at[wave, :, :, 0], field.at[wave], arrived.at[2 * wave + 1]
            ),
        ]
    for copy in copies:
        copy.start()
    tile_row = lax.axis_index("gx")
    block = lax.axis_index("gy")
    copies[0].wait()

    def put_count(tile, carry):
        at = lax.broadcasted_iota(jnp.int32, rows.shape, 1)
        count = jnp.sum(jnp.where(at == tile, rows[...], 0), axis=1, keepdims=True)
        counts[tile] = jnp.broadcast_to(count, counts.shape[1:])
        return carry

    over_tiles(tiles, put_count, 0)
    row = lax.broadcasted_iota(jnp.int32, (2 * focus, polars * height), 1)
    row = block * height + lax.rem(row, height)
    inner = []
    own = []
    for wave in range(waves):
        copies[2 * wave + 1].wait()
        parts = []
        for part in range(2):
            value = kern[wave, part, tile_row].astype(jnp.float32)
            parts.append(diagonal(one_block(value, block, side // height), polars))
        own.append(twice(jnp.concatenate(parts, axis=0).astype(kern.dtype), 1))
        copies[2 * wave + 2].wait()

        def add_tile(tile, value):
            planes = [field[wave, :, part, tile] for part in range(2)]
            planes = [plane.reshape(polars * height, side) for plane in planes]
            product = dot(
                jnp.concatenate(tile_kern(kern, wave, tile), axis=1),
                jnp.concatenate(planes, axis=1),
                (1, 1),
            )
            count = jnp.broadcast_to(counts[tile, :1, : polars * height], product.shape)
            return value + jnp.where(row < count, product, 0.0)

        zero = jnp.zeros((2 * focus, polars * height), jnp.float32)
        inner.append(over_tiles(tiles, add_tile, zero))
    for wave in range(waves):
        both = dot(jnp.concatenate(two_terms(inner[wave]), axis=1), own[wave], (1, 1))
        real, imag = both[:, : polars * focus], both[:, polars * focus :]
        focal = [real[:focus] - imag[focus:], real[focus:] + imag[:focus]]
        share[wave] = jnp.concatenate(focal, axis=0).astype(share.dtype)


def turned_strip(planes, block, blocks):
    rows = [
        jnp.concatenate([one_block(plane, block, blocks) for plane in pair], axis=1)
        for pair in planes
    ]
    return turn(jnp.concatenate(rows, axis=0).astype(jnp.bfloat16))


def live_planes(field, counts, wave, tile):
    polars, height, side = field.shape[1], field.shape[4], field.shape[5]
    live = live_rows(counts[tile, :1], (height, side))
    return [
        [
            jnp.where(live, field[wave, polar, part, tile].astype(jnp.float32), 0.0)
            for part in range(2)
        ]
        for polar in range(polars)
    ]


def strip_kernel(field, counts, *strips):
    waves, _, _, tiles, height, side = field.shape
    blocks = side // height
    block = lax.axis_index("gy")

    def one_tile(tile, carry):
        for wave in range(waves):
            planes = live_planes(field, counts, wave, tile)
            for distance, strip in enumerate(strips, 1):
                strip[wave, tile] = turned_strip(planes, block ^ distance, blocks)
        return carry

    over_tiles(tiles, one_tile, 0)


def layout_kernel(field, kern, counts, target, goal, row_kern, turn_kern, both_kern, own_strip):
    waves, polars, _, tiles, height, side = field.shape
    blocks = side // height
    block = lax.axis_index("gy")
    tile_row = lax.axis_index("gx")
    for wave in range(waves):
        goal[wave] = jnp.concatenate([target[wave].T] * polars, axis=1)
        for part in range(2):
            value = kern[wave, part, tile_row].astype(jnp.float32)
            columns = [
                diagonal(one_block(value, block ^ distance, blocks), polars)
                for distance in range(blocks)
            ]
            rows = pl.ds(part * polars * value.shape[0], polars * value.shape[0])
            row_kern[wave, rows] = jnp.concatenate(columns, axis=1).astype(kern.dtype)

    def one_tile(tile, carry):
        for wave in range(waves):
            parts = tile_kern(kern, wave, tile)
            both_kern[wave, tile] = jnp.concatenate(parts, axis=1)
            parts = [one_block(part.astype(jnp.float32), block, blocks) for part in parts]
            turned = turn(jnp.concatenate(parts, axis=1).astype(kern.dtype))
            turn_kern[wave, tile] = twice(turned, 1)
            planes = live_planes(field, counts, wave, tile)
            own_strip[wave, tile] = turned_strip(planes, block, blocks)
        return carry

    over_tiles(tiles, one_tile, 0)


def crossed_kernel(scale, blocks, row_kern, turn_kern, goal, *refs):
    strips, refs = refs[:blocks], refs[blocks:]
    shares, (intensity, near, crossed) = refs[:-3], refs[-3:]
    waves, tiles, height, width = strips[0].shape
    height = height // 2
    polars = width // height
    focus = goal.shape[1]
    block = lax.axis_index("gy")
    sides = []
    for wave in range(waves):
        focal = total([share[wave].astype(jnp.float32) for share in shares])
        real, imag = focal[:focus], focal[focus:]
        power = real * real + imag * imag
        power = sum(pltpu.roll(power, polar * focus, 1) for polar in range(polars))
        intensity[wave] = power
        excess = power - goal[wave]
        real, imag = excess * real, excess * imag
        upright = jnp.concatenate([real, imag], axis=0)
        turned = jnp.concatenate([imag, -real], axis=0)
        terms = two_terms(jnp.concatenate([upright, turned], axis=1))
        row = dot(jnp.concatenate(terms, axis=1), twice(row_kern[wave], 0), (1, 0))
        sides.append(jnp.concatenate(two_terms(row), axis=0))
        near[wave] = sides[wave]

    def add_tile(distance, carry):
        tile = lax.axis_index("gx") ^ distance
        value = jnp.zeros((2 * height, blocks * width), jnp.float32)
        for wave in range(waves):
            back = dot(turn_kern[wave, tile], sides[wave], (1, 0))
            strip = jnp.concatenate([strip[wave, tile] for strip in strips], axis=1)
            value += back * strip.astype(jnp.float32)
        value = (value[:height] + value[height:]) * scale
        parts = []
        for apart in range(blocks):
            part = value[:, apart * width : (apart + 1) * width]
            parts.append(sum(part[:, at * height : (at + 1) * height] for at in range(polars)))
        columns = []
        for index in range(blocks):
            column = parts[0]
            for apart in range(1, blocks):
                column = jnp.where((block ^ apart) == index, parts[apart], column)
            columns.append(column)
        crossed[distance] = jnp.concatenate(columns, axis=1).astype(crossed.dtype)
        return carry

    over_tiles(tiles, add_tile, 0)


def straight_kernel(scale, field, counts, both_kern, near, gradient):
    waves, polars, _, tiles, height, side = field.shape
    sides = []
    for wave in range(waves):
        sides.append(turn(near[wave, :, : polars * height]))

    def add_tile(distance, carry):
        tile = lax.axis_index("gx") ^ distance
        term = jnp.zeros((height, side), jnp.float32)
        for wave in range(waves):
            back = dot(sides[wave], twice(both_kern[wave, tile], 0), (1, 0))
            back = back.reshape(polars, height, 2 * side)
            for polar in range(polars):
                for part in range(2):
                    plane = field[wave, polar, part, tile].astype(jnp.float32)
                    term += back[polar, :, part * side : (part + 1) * side] * plane
        live = live_rows(counts[tile, :1], (height, side))
        gradient[distance] = jnp.where(live, term * scale, 0.0)
        return carry

    over_tiles(tiles, add_tile, 0)


def call(kernel, out_shape, scratch, args, spaces):
    return pl.pallas_call(
        kernel,
        out_shape=out_shape,
        in_specs=[pl.BlockSpec(memory_space=space) for space in spaces],
        out_specs=[pl.BlockSpec(memory_space=pltpu.VMEM)] * len(out_shape),
        scratch_shapes=scratch,
        compiler_params=pltpu.CompilerParams(vmem_limit_bytes=VMEM),
    )(*args)


def pairs(count, distance):
    return [(device, device ^ distance) for device in range(count)]


def partners(value, axis, count):
    came = {d: lax.ppermute(value(d), axis, pairs(count, d)) for d in range(count - 1, 0, -1)}
    return [came[d] for d in range(1, count)]


def crosswise(value, mesh):
    count, cores = mesh.shape["gx"], mesh.shape["wa"]

    def routes(distance):
        odd = distance % 2 == 1
        return [
            (
                device * cores + core,
                (device ^ distance) * cores + (cores - 1 - core if odd else core),
            )
            for device in range(count)
            for core in range(cores)
        ]

    came = {d: lax.ppermute(value(d), ("gx", "wa"), routes(d)) for d in range(count - 1, 0, -1)}
    return [came[d] for d in range(1, count)]


def total(terms):
    while len(terms) > 1:
        terms = [first + second for first, second in zip(terms[::2], terms[1::2])]
    return terms[0]


def rounded(value):
    return lax.reduce_precision(value, 8, 7)


def in_order(came, me):
    count = came.shape[0]
    rest = came.shape[1:]
    bit = 1
    while bit < count:
        split = came.reshape((count // (2 * bit), 2, bit) + rest)
        came = jnp.where((me & bit) != 0, split[:, ::-1], split).reshape((count,) + rest)
        bit *= 2
    return came


def make(mesh):
    count_x = mesh.shape["gx"]
    count_y = mesh.shape["gy"]

    def on_device(field, active_rows, kern, target):
        tile_row = lax.axis_index("gx")
        waves, polars = field.shape[0], field.shape[1]
        tiles = field.shape[4]
        rows_dev = field.shape[5]
        side = field.shape[6]
        focus = kern.shape[3]
        shape = (waves, 2 * focus, polars * focus)
        share, near_field, near_kern, counts = call(
            share_kernel,
            [
                jax.ShapeDtypeStruct(shape, jnp.bfloat16),
                jax.ShapeDtypeStruct(field.shape[:3] + field.shape[4:], field.dtype),
                jax.ShapeDtypeStruct(kern.shape, kern.dtype),
                jax.ShapeDtypeStruct((tiles, 8, side), jnp.int32),
            ],
            [
                pltpu.VMEM(active_rows.shape, jnp.int32),
                pltpu.SemaphoreType.DMA((2 * waves + 1,)),
            ],
            [
                pltpu.with_memory_space_constraint(operand, pltpu.HBM)
                for operand in (active_rows, field, kern)
            ],
            [pltpu.HBM] * 3,
        )
        shares = [share] + partners(lambda d: share, "gy", count_y)
        share = total([term.astype(jnp.float32) for term in shares]).astype(jnp.bfloat16)
        strip_shape = (waves, tiles, 2 * rows_dev, polars * rows_dev)
        strips = call(
            strip_kernel,
            [jax.ShapeDtypeStruct(strip_shape, field.dtype)] * (count_y - 1),
            [],
            (near_field, counts),
            [pltpu.VMEM] * 2,
        )
        strips = partners(lambda d: strips[d - 1], "gy", count_y)
        shares = [share] + partners(lambda d: share, "gx", count_x)
        shares = shares[::-1]
        shape = (tiles, rows_dev, side)
        goal, row_kern, turn_kern, both_kern, own_strip = call(
            layout_kernel,
            [
                jax.ShapeDtypeStruct((waves, focus, polars * focus), target.dtype),
                jax.ShapeDtypeStruct((waves, 2 * polars * focus, polars * side), kern.dtype),
                jax.ShapeDtypeStruct((waves, tiles, 2 * rows_dev, 4 * focus), kern.dtype),
                jax.ShapeDtypeStruct((waves, tiles, 2 * focus, 2 * side), kern.dtype),
                jax.ShapeDtypeStruct(strip_shape, field.dtype),
            ],
            [],
            (near_field, near_kern, counts, target),
            [pltpu.VMEM] * 4,
        )
        scale = tiles * side / focus
        power, near, crossed = call(
            functools.partial(crossed_kernel, scale, count_y),
            [
                jax.ShapeDtypeStruct((waves, focus, polars * focus), jnp.float32),
                jax.ShapeDtypeStruct((waves, 4 * focus, polars * side), jnp.bfloat16),
                jax.ShapeDtypeStruct(shape, jnp.bfloat16),
            ],
            [],
            (row_kern, turn_kern, goal, own_strip, *strips, *shares),
            [pltpu.VMEM] * (3 + count_x + count_y),
        )
        (gradient,) = call(
            functools.partial(straight_kernel, scale),
            [jax.ShapeDtypeStruct(shape, jnp.float32)],
            [],
            (near_field, counts, both_kern, near),
            [pltpu.VMEM] * 4,
        )
        came = [crossed[0]] + crosswise(lambda d: crossed[d], mesh)
        own = rounded(gradient + jnp.stack(came).astype(jnp.float32))
        other = lax.ppermute(own.astype(jnp.bfloat16), "wa", pairs(2, 1))
        design_grad = in_order(0.5 * (own + other.astype(jnp.float32)), tile_row)
        intensity = jnp.swapaxes(power[:, :, :focus], 1, 2)
        return (design_grad[None], intensity)

    return on_device


def solution(mesh):
    placed = (
        P("wa", "cand", None, "gx", None, "gy", None),
        P("gx", None),
        P("wa", None, None, None, None),
        P("wa", None, None),
    )
    return jax.shard_map(
        make(mesh),
        mesh=mesh,
        in_specs=placed,
        out_specs=(P("gx", "cand", "gy", None), P("wa", "cand", None)),
        check_vma=False,
    )
```

profile of v0, /device:TPU:0, one launch (start us, length us, event | category | flops | bytes accessed | tf_op | source)
XLA Modules:
  0.0 25.6 jit_solution(2713207290940341379)
XLA Ops:
  0.6 1.9 %shard_map.59 = (bf16[2,128,128]{2,1,0:T(8,128)(2,1)S(1)}, bf16[2,2,2,4,64,128]{5,4,3,2,1,0:T(8,128)(2,1)S(1)}, bf16[2,2,4,64,128]{4,3,2,1,0:T(8,128)(2,1)S(1)}, s32[4,8,128]{2,1,0:T(8,128)S(1)}) custom-call(s32[1,4]{1,0:T(1,128)} %rows_far.1, bf16[2,2,2,1,4,64,128]{6,5,4,3,2,1,0:T(8,128)(2,1)} %field_far.1, bf16[2,2,4,64,128]{4,3,2,1,0:T(8,128)(2,1)} %kern_far.1), custom_call_target="tpu_custom_call" | custom-call | tf_op jit(solution)/shard_map/pallas_call | solution.py:262
  2.5 3.0 %collective-permute-start.1 = (bf16[2,128,128]{2,1,0:T(8,128)(2,1)S(1)}, bf16[2,128,128]{2,1,0:T(8,128)(2,1)S(1)}, u32[]{:S(2)}, u32[]{:S(2)}) collective-permute-start(bf16[2,128,128]{2,1,0:T(8,128)(2,1)S(1)} %get-tuple-element.22), channel_id=1, source_target_pairs={{0,2},{2,0},{1,3},{3,1},{4,6},{6,4},{5,7},{7,5},{8,10},{10,8},{9,1... | collective-permute-start | bytes 196616 | tf_op jit(solution)/shard_map/ppermute | solution.py:277
  5.5 0.5 %shard_map.61 = bf16[2,4,128,128]{3,2,1,0:T(8,128)(2,1)S(1)} custom-call(bf16[2,2,2,4,64,128]{5,4,3,2,1,0:T(8,128)(2,1)S(1)} %get-tuple-element.14.field, s32[4,8,128]{2,1,0:T(8,128)S(1)} %get-tuple-element.15.counts), custom_call_target="tpu_custom_call" | custom-call | tf_op jit(solution)/shard_map/pallas_call | solution.py:262
  6.0 0.0 copy-start
  6.0 0.1 collective-permute-start
  6.1 1.9 %collective-permute-done.1 = bf16[2,128,128]{2,1,0:T(8,128)(2,1)S(1)} collective-permute-done((bf16[2,128,128]{2,1,0:T(8,128)(2,1)S(1)}, bf16[2,128,128]{2,1,0:T(8,128)(2,1)S(1)}, u32[]{:S(2)}, u32[]{:S(2)}) %collective-permute-start.1) | collective-permute-done | bytes 65568 | tf_op jit(solution)/shard_map/ppermute | solution.py:277
  8.0 4.0 %collective-permute-start.2 = (bf16[2,128,128]{2,1,0:T(8,128)(2,1)S(1)}, bf16[2,128,128]{2,1,0:T(8,128)(2,1)S(1)}, u32[]{:S(2)}, u32[]{:S(2)}) collective-permute-start(bf16[2,128,128]{2,1,0:T(8,128)(2,1)S(1)} %add_convert_fusion.refs_5_), channel_id=1, source_target_pairs={{0,12},{4,8},{8,4},{12,0},{1,13},{5,9},{9,5},{13,1},{2,14},{6,10},... | collective-permute-start | bytes 196616 | tf_op jit(solution)/shard_map/ppermute | solution.py:277
  12.0 0.0 collective-permute-start.3
  12.1 0.6 %collective-permute-start.4 = (bf16[2,128,128]{2,1,0:T(8,128)(2,1)S(1)}, bf16[2,128,128]{2,1,0:T(8,128)(2,1)S(1)}, u32[]{:S(2)}, u32[]{:S(2)}) collective-permute-start(bf16[2,128,128]{2,1,0:T(8,128)(2,1)S(1)} %add_convert_fusion.refs_5_), channel_id=1, source_target_pairs={{0,4},{4,0},{8,12},{12,8},{1,5},{5,1},{9,13},{13,9},{2,6},{6,2},{1... | collective-permute-start | bytes 196616 | tf_op jit(solution)/shard_map/ppermute | solution.py:277
  12.7 0.0 copy-done
  12.7 1.8 %shard_map.60 = (f32[2,64,128]{2,1,0:T(8,128)S(1)}, bf16[2,256,256]{2,1,0:T(8,128)(2,1)S(1)}, bf16[2,4,128,256]{3,2,1,0:T(8,128)(2,1)S(1)}, bf16[2,4,128,256]{3,...) custom-call(bf16[2,2,2,4,64,128]{5,4,3,2,1,0:T(8,128)(2,1)S(1)} %get-tuple-element.14.field, ...), custom_call_target="tpu_custom_call" | custom-call | tf_op jit(solution)/shard_map/pallas_call | solution.py:262
  14.5 0.0 collective-permute-done.2.refs_2_
  14.5 2.7 %collective-permute-done.3.refs_3_ = bf16[2,128,128]{2,1,0:T(8,128)(2,1)S(1)} collective-permute-done((bf16[2,128,128]{2,1,0:T(8,128)(2,1)S(1)}, bf16[2,128,128]{2,1,0:T(8,128)(2,1)S(1)}, u32[]{:S(2)}, u32[]{:S(2)}) %collective-permute-start.3) | collective-permute-done | bytes 65568 | tf_op jit(solution)/shard_map/ppermute | solution.py:277
  17.2 0.0 collective-permute-done.4.refs_4_
  17.2 0.0 collective-permute-done.refs_1_
  17.2 0.7 %shard_map.62 = (f32[2,64,128]{2,1,0:T(8,128)S(1)}, bf16[2,256,256]{2,1,0:T(8,128)(2,1)S(1)}, bf16[4,64,128]{2,1,0:T(8,128)(2,1)S(1)}) custom-call(bf16[2,256,256]{2,1,0:T(8,128)(2,1)S(1)} %get-tuple-element.18.row_kern, bf16[2,4,128,256]{3,2,1,0:T(8,128)(2,1)S(1)} %get-tuple-element.19.turn_kern, f32[2,64,128]{2,1,0:T(8,128)S(1)} %get-tuple-element.20.goal, ...), custom_call_target="tpu_custom_call" | custom-call | tf_op jit(solution)/shard_map/pallas_call | solution.py:262
  18.0 0.1 collective-permute-start.7
  18.1 2.1 %collective-permute-start.6 = (bf16[64,128]{1,0:T(8,128)(2,1)S(1)}, bf16[64,128]{1,0:T(8,128)(2,1)S(1)}, u32[]{:S(2)}, u32[]{:S(2)}) collective-permute-start(bf16[64,128]{1,0:T(8,128)(2,1)S(1)} %get-tuple-element.30), channel_id=1, source_target_pairs={{0,8},{1,9},{4,12},{5,13},{8,0},{9,1},{12,4},{13,5},{2,10},{3,11},... | collective-permute-start | bytes 49160 | tf_op jit(solution)/shard_map/ppermute | solution.py:295
  20.1 1.7 %collective-permute-start.5 = (bf16[64,128]{1,0:T(8,128)(2,1)S(1)}, bf16[64,128]{1,0:T(8,128)(2,1)S(1)}, u32[]{:S(2)}, u32[]{:S(2)}) collective-permute-start(bf16[64,128]{1,0:T(8,128)(2,1)S(1)} %get-tuple-element.31), channel_id=1, source_target_pairs={{0,5},{1,4},{4,1},{5,0},{8,13},{9,12},{12,9},{13,8},{2,7},{3,6},{6... | collective-permute-start | bytes 49160 | tf_op jit(solution)/shard_map/ppermute | solution.py:295
  21.9 0.4 %shard_map.63 = f32[4,64,128]{2,1,0:T(8,128)S(1)} custom-call(bf16[2,2,2,4,64,128]{5,4,3,2,1,0:T(8,128)(2,1)S(1)} %get-tuple-element.14.field, s32[4,8,128]{2,1,0:T(8,128)S(1)} %get-tuple-element.15.counts, bf16[2,4,128,256]{3,2,1,0:T(8,128)(2,1)S(1)} %get-tuple-element.17.both_kern, bf16[2,256,256]{2,1,0:T(8,128)(2,1)S(1)} %get-tuple-element.23.near), custom_call_target="tpu_custom_call" | custom-call | tf_op jit(solution)/shard_map/pallas_call | solution.py:262
  22.3 0.7 %collective-permute-done.7 = bf16[64,128]{1,0:T(8,128)(2,1)S(1)} collective-permute-done((bf16[64,128]{1,0:T(8,128)(2,1)S(1)}, bf16[64,128]{1,0:T(8,128)(2,1)S(1)}, u32[]{:S(2)}, u32[]{:S(2)}) %collective-permute-start.7) | collective-permute-done | bytes 16416 | tf_op jit(solution)/shard_map/ppermute | solution.py:295
  23.0 0.1 collective-permute-done.6
  23.1 0.2 collective-permute-done.5
  23.3 0.6 %collective-permute-start.8 = (bf16[4,64,128]{2,1,0:T(8,128)(2,1)S(1)}, bf16[4,64,128]{2,1,0:T(8,128)(2,1)S(1)}, u32[]{:S(2)}, u32[]{:S(2)}) collective-permute-start(bf16[4,64,128]{2,1,0:T(8,128)(2,1)S(1)} %fusion.1), channel_id=1, source_target_pairs={{0,1},{1,0},{2,3},{3,2},{4,5},{5,4},{6,7},{7,6},{8,9},{9,8},{10,11... | collective-permute-start | bytes 196616 | tf_op jit(solution)/shard_map/ppermute | solution.py:398
  23.9 0.7 %copy.6 = f32[2,64,64]{2,1,0:T(8,128)} copy(f32[2,64,64]{1,2,0:T(8,128)S(1)} %slice_bitcast_fusion) | data formatting | bytes 65536
  24.6 0.2 collective-permute-done.8
  24.9 0.7 %reverse_select_fusion = f32[1,2,2,64,128]{4,3,2,1,0:T(8,128)} fusion(f32[1,2,2,64,128]{4,3,2,1,0:T(8,128)S(1)} %fusion, pred[]{:T(512)S(6)} %ne.6), kind=kLoop, calls=%fused_computation | loop fusion | flops 32768 | bytes 262145 | tf_op jit(solution)/shard_map/jit(_where)/select_n | solution.py:315
  (6 shorter events, 0.1 us)
Async XLA Ops:
  2.5 5.5 %collective-permute-start.1 = (bf16[2,128,128]{2,1,0:T(8,128)(2,1)S(1)}, bf16[2,128,128]{2,1,0:T(8,128)(2,1)S(1)}, u32[]{:S(2)}, u32[]{:S(2)}) collective-permute-start(bf16[2,128,128]{2,1,0:T(8,128)(2,1)S(1)} %get-tuple-element.22), channel_id=1, source_target_pairs={{0,2},{2,0},{1,3},{3,1},{4,6},{6,4},{5,7},{7,5},{8,10},{10,8},{9,1... | collective-permute-start | bytes 196616 | tf_op jit(solution)/shard_map/ppermute | solution.py:277
  6.0 6.7 %copy-start = (f32[2,64,64]{2,1,0:T(8,128)S(1)}, f32[2,64,64]{2,1,0:T(8,128)}, u32[]{:S(2)}) copy-start(f32[2,64,64]{2,1,0:T(8,128)} %target.1) | copy-start | bytes 98308
  6.0 11.2 %collective-permute-start = (bf16[2,4,128,128]{3,2,1,0:T(8,128)(2,1)S(1)}, bf16[2,4,128,128]{3,2,1,0:T(8,128)(2,1)S(1)}, u32[]{:S(2)}, u32[]{:S(2)}) collective-permute-start(bf16[2,4,128,128]{3,2,1,0:T(8,128)(2,1)S(1)} %shard_map.61), channel_id=1, source_target_pairs={{0,2},{2,0},{1,3},{3,1},{4,6},{6,4},{5,7},{7,5},{8,10},{10,8},{9,1... | collective-permute-start | bytes 786440 | tf_op jit(solution)/shard_map/ppermute | solution.py:277
  8.0 6.4 %collective-permute-start.2 = (bf16[2,128,128]{2,1,0:T(8,128)(2,1)S(1)}, bf16[2,128,128]{2,1,0:T(8,128)(2,1)S(1)}, u32[]{:S(2)}, u32[]{:S(2)}) collective-permute-start(bf16[2,128,128]{2,1,0:T(8,128)(2,1)S(1)} %add_convert_fusion.refs_5_), channel_id=1, source_target_pairs={{0,12},{4,8},{8,4},{12,0},{1,13},{5,9},{9,5},{13,1},{2,14},{6,10},... | collective-permute-start | bytes 196616 | tf_op jit(solution)/shard_map/ppermute | solution.py:277
  12.0 5.2 %collective-permute-start.3 = (bf16[2,128,128]{2,1,0:T(8,128)(2,1)S(1)}, bf16[2,128,128]{2,1,0:T(8,128)(2,1)S(1)}, u32[]{:S(2)}, u32[]{:S(2)}) collective-permute-start(bf16[2,128,128]{2,1,0:T(8,128)(2,1)S(1)} %add_convert_fusion.refs_5_), channel_id=1, source_target_pairs={{0,8},{4,12},{8,0},{12,4},{1,9},{5,13},{9,1},{13,5},{2,10},{6,14},... | collective-permute-start | bytes 196616 | tf_op jit(solution)/shard_map/ppermute | solution.py:277
  12.1 5.2 %collective-permute-start.4 = (bf16[2,128,128]{2,1,0:T(8,128)(2,1)S(1)}, bf16[2,128,128]{2,1,0:T(8,128)(2,1)S(1)}, u32[]{:S(2)}, u32[]{:S(2)}) collective-permute-start(bf16[2,128,128]{2,1,0:T(8,128)(2,1)S(1)} %add_convert_fusion.refs_5_), channel_id=1, source_target_pairs={{0,4},{4,0},{8,12},{12,8},{1,5},{5,1},{9,13},{13,9},{2,6},{6,2},{1... | collective-permute-start | bytes 196616 | tf_op jit(solution)/shard_map/ppermute | solution.py:277
  18.0 5.0 %collective-permute-start.7 = (bf16[64,128]{1,0:T(8,128)(2,1)S(1)}, bf16[64,128]{1,0:T(8,128)(2,1)S(1)}, u32[]{:S(2)}, u32[]{:S(2)}) collective-permute-start(bf16[64,128]{1,0:T(8,128)(2,1)S(1)} %get-tuple-element.29), channel_id=1, source_target_pairs={{0,13},{1,12},{4,9},{5,8},{8,5},{9,4},{12,1},{13,0},{2,15},{3,14},... | collective-permute-start | bytes 49160 | tf_op jit(solution)/shard_map/ppermute | solution.py:295
  18.1 5.0 %collective-permute-start.6 = (bf16[64,128]{1,0:T(8,128)(2,1)S(1)}, bf16[64,128]{1,0:T(8,128)(2,1)S(1)}, u32[]{:S(2)}, u32[]{:S(2)}) collective-permute-start(bf16[64,128]{1,0:T(8,128)(2,1)S(1)} %get-tuple-element.30), channel_id=1, source_target_pairs={{0,8},{1,9},{4,12},{5,13},{8,0},{9,1},{12,4},{13,5},{2,10},{3,11},... | collective-permute-start | bytes 49160 | tf_op jit(solution)/shard_map/ppermute | solution.py:295
  20.1 3.2 %collective-permute-start.5 = (bf16[64,128]{1,0:T(8,128)(2,1)S(1)}, bf16[64,128]{1,0:T(8,128)(2,1)S(1)}, u32[]{:S(2)}, u32[]{:S(2)}) collective-permute-start(bf16[64,128]{1,0:T(8,128)(2,1)S(1)} %get-tuple-element.31), channel_id=1, source_target_pairs={{0,5},{1,4},{4,1},{5,0},{8,13},{9,12},{12,9},{13,8},{2,7},{3,6},{6... | collective-permute-start | bytes 49160 | tf_op jit(solution)/shard_map/ppermute | solution.py:295
  23.3 1.5 %collective-permute-start.8 = (bf16[4,64,128]{2,1,0:T(8,128)(2,1)S(1)}, bf16[4,64,128]{2,1,0:T(8,128)(2,1)S(1)}, u32[]{:S(2)}, u32[]{:S(2)}) collective-permute-start(bf16[4,64,128]{2,1,0:T(8,128)(2,1)S(1)} %fusion.1), channel_id=1, source_target_pairs={{0,1},{1,0},{2,3},{3,2},{4,5},{5,4},{6,7},{7,6},{8,9},{9,8},{10,11... | collective-permute-start | bytes 196616 | tf_op jit(solution)/shard_map/ppermute | solution.py:398
where the time goes:
time: 25.7 us; the launch traced here: 25.6 us
  starting transfers between devices  12.2 us (47%)
  waiting for transfers between devices  5.8 us (23%)
  Pallas kernels  5.33 us (21%)
  other arithmetic  0.75 us (3%)
  local copies, waits for them, and re-layouts  0.73 us (3%)
  between operations  0.71 us (3%)
    ppermute x5, starting transfers between devices, partners(): lax.ppermute(value(d), axis, pairs(count, d))  7.75 us
    pallas_call x5, Pallas kernels, call(): pl.pallas_call(kernel, out_shape=out_shape, in_specs=[pl.BlockSpec(memory...  5.33 us
    ppermute x5, waiting for transfers between devices, partners(): lax.ppermute(value(d), axis, pairs(count, d))  4.62 us
    ppermute x3, starting transfers between devices, crosswise(): lax.ppermute(value(d), ('gx', 'wa'), routes(d))  3.89 us
    ppermute x3, waiting for transfers between devices, crosswise(): lax.ppermute(value(d), ('gx', 'wa'), routes(d))  1 us
    unnamed x3, local copies, waits for them, and re-layouts  0.72 us
    select_n x1, other arithmetic, in_order(): jnp.where(me & bit != 0, split[:, ::-1], split).reshape((count,) + rest)  0.67 us
    ppermute x1, starting transfers between devices, on_device(): other = lax.ppermute(own.astype(jnp.bfloat16), 'wa', pairs(2, 1))  0.6 us
  transfers between devices with their start and end apart: 9, of which 6 were waited for; matrix products, arithmetic and copies ran while one was open for 3% of the time, Pallas kernels for 11%

commit v1 on v0

--- a/solution.py
+++ b/solution.py
@@ -394,9 +394,9 @@
             [pltpu.VMEM] * 4,
         )
         came = [crossed[0]] + crosswise(lambda d: crossed[d], mesh)
-        own = rounded(gradient + jnp.stack(came).astype(jnp.float32))
+        own = rounded(in_order(gradient + jnp.stack(came).astype(jnp.float32), tile_row))
         other = lax.ppermute(own.astype(jnp.bfloat16), "wa", pairs(2, 1))
-        design_grad = in_order(0.5 * (own + other.astype(jnp.float32)), tile_row)
+        design_grad = 0.5 * (own + other.astype(jnp.float32))
         intensity = jnp.swapaxes(power[:, :, :focus], 1, 2)
         return (design_grad[None], intensity)
 

time: 25.7 us -> 25.7 us (level)
    select_n x1 -> x0, other arithmetic: 0.67 us -> none  [in_order(): jnp.where(me & bit != 0, split[:, ::-1], split).reshape((count,) + rest)]
    mul x1, other arithmetic: 0.03 us -> 0.67 us  [on_device(): design_grad = 0.5 * (own + other.astype(jnp.float32))]
where the time goes in v1:
time: 25.7 us; the launch traced here: 25.6 us
  starting transfers between devices  12.2 us (47%)
  waiting for transfers between devices  5.8 us (23%)
  Pallas kernels  5.33 us (21%)
  other arithmetic  0.75 us (3%)
  local copies, waits for them, and re-layouts  0.73 us (3%)
  between operations  0.72 us (3%)
    ppermute x5, starting transfers between devices, partners(): lax.ppermute(value(d), axis, pairs(count, d))  7.75 us
    pallas_call x5, Pallas kernels, call(): pl.pallas_call(kernel, out_shape=out_shape, in_specs=[pl.BlockSpec(memory...  5.33 us
    ppermute x5, waiting for transfers between devices, partners(): lax.ppermute(value(d), axis, pairs(count, d))  4.62 us
    ppermute x3, starting transfers between devices, crosswise(): lax.ppermute(value(d), ('gx', 'wa'), routes(d))  3.89 us
    ppermute x3, waiting for transfers between devices, crosswise(): lax.ppermute(value(d), ('gx', 'wa'), routes(d))  1 us
    unnamed x3, local copies, waits for them, and re-layouts  0.72 us
    mul x1, other arithmetic, on_device(): design_grad = 0.5 * (own + other.astype(jnp.float32))  0.67 us
    ppermute x1, starting transfers between devices, on_device(): other = lax.ppermute(own.astype(jnp.bfloat16), 'wa', pairs(2, 1))  0.6 us
  transfers between devices with their start and end apart: 9, of which 6 were waited for; matrix products, arithmetic and copies ran while one was open for 3% of the time, Pallas kernels for 11%

profile of v1, /device:TPU:0, one launch (start us, length us, event | category | flops | bytes accessed | tf_op | source)
XLA Modules:
  0.0 25.6 jit_solution(6162161964282938169)
XLA Ops:
  0.6 1.9 %shard_map.59 = (bf16[2,128,128]{2,1,0:T(8,128)(2,1)S(1)}, bf16[2,2,2,4,64,128]{5,4,3,2,1,0:T(8,128)(2,1)S(1)}, bf16[2,2,4,64,128]{4,3,2,1,0:T(8,128)(2,1)S(1)}, s32[4,8,128]{2,1,0:T(8,128)S(1)}) custom-call(s32[1,4]{1,0:T(1,128)} %rows_far.1, bf16[2,2,2,1,4,64,128]{6,5,4,3,2,1,0:T(8,128)(2,1)} %field_far.1, bf16[2,2,4,64,128]{4,3,2,1,0:T(8,128)(2,1)} %kern_far.1), custom_call_target="tpu_custom_call" | custom-call | tf_op jit(solution)/shard_map/pallas_call | solution.py:262
  2.5 3.0 %collective-permute-start.1 = (bf16[2,128,128]{2,1,0:T(8,128)(2,1)S(1)}, bf16[2,128,128]{2,1,0:T(8,128)(2,1)S(1)}, u32[]{:S(2)}, u32[]{:S(2)}) collective-permute-start(bf16[2,128,128]{2,1,0:T(8,128)(2,1)S(1)} %get-tuple-element.22), channel_id=1, source_target_pairs={{0,2},{2,0},{1,3},{3,1},{4,6},{6,4},{5,7},{7,5},{8,10},{10,8},{9,1... | collective-permute-start | bytes 196616 | tf_op jit(solution)/shard_map/ppermute | solution.py:277
  5.5 0.5 %shard_map.61 = bf16[2,4,128,128]{3,2,1,0:T(8,128)(2,1)S(1)} custom-call(bf16[2,2,2,4,64,128]{5,4,3,2,1,0:T(8,128)(2,1)S(1)} %get-tuple-element.14.field, s32[4,8,128]{2,1,0:T(8,128)S(1)} %get-tuple-element.15.counts), custom_call_target="tpu_custom_call" | custom-call | tf_op jit(solution)/shard_map/pallas_call | solution.py:262
  6.0 0.0 copy-start
  6.0 0.1 collective-permute-start
  6.1 1.9 %collective-permute-done.1 = bf16[2,128,128]{2,1,0:T(8,128)(2,1)S(1)} collective-permute-done((bf16[2,128,128]{2,1,0:T(8,128)(2,1)S(1)}, bf16[2,128,128]{2,1,0:T(8,128)(2,1)S(1)}, u32[]{:S(2)}, u32[]{:S(2)}) %collective-permute-start.1) | collective-permute-done | bytes 65568 | tf_op jit(solution)/shard_map/ppermute | solution.py:277
  8.0 4.0 %collective-permute-start.2 = (bf16[2,128,128]{2,1,0:T(8,128)(2,1)S(1)}, bf16[2,128,128]{2,1,0:T(8,128)(2,1)S(1)}, u32[]{:S(2)}, u32[]{:S(2)}) collective-permute-start(bf16[2,128,128]{2,1,0:T(8,128)(2,1)S(1)} %add_convert_fusion.refs_5_), channel_id=1, source_target_pairs={{0,12},{4,8},{8,4},{12,0},{1,13},{5,9},{9,5},{13,1},{2,14},{6,10},... | collective-permute-start | bytes 196616 | tf_op jit(solution)/shard_map/ppermute | solution.py:277
  12.0 0.0 collective-permute-start.3
  12.1 0.6 %collective-permute-start.4 = (bf16[2,128,128]{2,1,0:T(8,128)(2,1)S(1)}, bf16[2,128,128]{2,1,0:T(8,128)(2,1)S(1)}, u32[]{:S(2)}, u32[]{:S(2)}) collective-permute-start(bf16[2,128,128]{2,1,0:T(8,128)(2,1)S(1)} %add_convert_fusion.refs_5_), channel_id=1, source_target_pairs={{0,4},{4,0},{8,12},{12,8},{1,5},{5,1},{9,13},{13,9},{2,6},{6,2},{1... | collective-permute-start | bytes 196616 | tf_op jit(solution)/shard_map/ppermute | solution.py:277
  12.7 0.0 copy-done
  12.7 1.8 %shard_map.60 = (f32[2,64,128]{2,1,0:T(8,128)S(1)}, bf16[2,256,256]{2,1,0:T(8,128)(2,1)S(1)}, bf16[2,4,128,256]{3,2,1,0:T(8,128)(2,1)S(1)}, bf16[2,4,128,256]{3,...) custom-call(bf16[2,2,2,4,64,128]{5,4,3,2,1,0:T(8,128)(2,1)S(1)} %get-tuple-element.14.field, ...), custom_call_target="tpu_custom_call" | custom-call | tf_op jit(solution)/shard_map/pallas_call | solution.py:262
  14.5 0.0 collective-permute-done.2.refs_2_
  14.5 2.7 %collective-permute-done.3.refs_3_ = bf16[2,128,128]{2,1,0:T(8,128)(2,1)S(1)} collective-permute-done((bf16[2,128,128]{2,1,0:T(8,128)(2,1)S(1)}, bf16[2,128,128]{2,1,0:T(8,128)(2,1)S(1)}, u32[]{:S(2)}, u32[]{:S(2)}) %collective-permute-start.3) | collective-permute-done | bytes 65568 | tf_op jit(solution)/shard_map/ppermute | solution.py:277
  17.2 0.0 collective-permute-done.4.refs_4_
  17.2 0.0 collective-permute-done.refs_1_
  17.2 0.7 %shard_map.62 = (f32[2,64,128]{2,1,0:T(8,128)S(1)}, bf16[2,256,256]{2,1,0:T(8,128)(2,1)S(1)}, bf16[4,64,128]{2,1,0:T(8,128)(2,1)S(1)}) custom-call(bf16[2,256,256]{2,1,0:T(8,128)(2,1)S(1)} %get-tuple-element.18.row_kern, bf16[2,4,128,256]{3,2,1,0:T(8,128)(2,1)S(1)} %get-tuple-element.19.turn_kern, f32[2,64,128]{2,1,0:T(8,128)S(1)} %get-tuple-element.20.goal, ...), custom_call_target="tpu_custom_call" | custom-call | tf_op jit(solution)/shard_map/pallas_call | solution.py:262
  18.0 0.1 collective-permute-start.7
  18.1 2.1 %collective-permute-start.6 = (bf16[64,128]{1,0:T(8,128)(2,1)S(1)}, bf16[64,128]{1,0:T(8,128)(2,1)S(1)}, u32[]{:S(2)}, u32[]{:S(2)}) collective-permute-start(bf16[64,128]{1,0:T(8,128)(2,1)S(1)} %get-tuple-element.30), channel_id=1, source_target_pairs={{0,8},{1,9},{4,12},{5,13},{8,0},{9,1},{12,4},{13,5},{2,10},{3,11},... | collective-permute-start | bytes 49160 | tf_op jit(solution)/shard_map/ppermute | solution.py:295
  20.1 1.7 %collective-permute-start.5 = (bf16[64,128]{1,0:T(8,128)(2,1)S(1)}, bf16[64,128]{1,0:T(8,128)(2,1)S(1)}, u32[]{:S(2)}, u32[]{:S(2)}) collective-permute-start(bf16[64,128]{1,0:T(8,128)(2,1)S(1)} %get-tuple-element.31), channel_id=1, source_target_pairs={{0,5},{1,4},{4,1},{5,0},{8,13},{9,12},{12,9},{13,8},{2,7},{3,6},{6... | collective-permute-start | bytes 49160 | tf_op jit(solution)/shard_map/ppermute | solution.py:295
  21.9 0.4 %shard_map.63 = f32[4,64,128]{2,1,0:T(8,128)S(1)} custom-call(bf16[2,2,2,4,64,128]{5,4,3,2,1,0:T(8,128)(2,1)S(1)} %get-tuple-element.14.field, s32[4,8,128]{2,1,0:T(8,128)S(1)} %get-tuple-element.15.counts, bf16[2,4,128,256]{3,2,1,0:T(8,128)(2,1)S(1)} %get-tuple-element.17.both_kern, bf16[2,256,256]{2,1,0:T(8,128)(2,1)S(1)} %get-tuple-element.23.near), custom_call_target="tpu_custom_call" | custom-call | tf_op jit(solution)/shard_map/pallas_call | solution.py:262
  22.3 0.7 %collective-permute-done.7 = bf16[64,128]{1,0:T(8,128)(2,1)S(1)} collective-permute-done((bf16[64,128]{1,0:T(8,128)(2,1)S(1)}, bf16[64,128]{1,0:T(8,128)(2,1)S(1)}, u32[]{:S(2)}, u32[]{:S(2)}) %collective-permute-start.7) | collective-permute-done | bytes 16416 | tf_op jit(solution)/shard_map/ppermute | solution.py:295
  23.0 0.1 collective-permute-done.6
  23.1 0.2 collective-permute-done.5
  23.4 0.6 %collective-permute-start.8 = (bf16[4,64,128]{2,1,0:T(8,128)(2,1)S(1)}, bf16[4,64,128]{2,1,0:T(8,128)(2,1)S(1)}, u32[]{:S(2)}, u32[]{:S(2)}) collective-permute-start(bf16[4,64,128]{2,1,0:T(8,128)(2,1)S(1)} %bitcast_convert_fusion), channel_id=1, source_target_pairs={{0,1},{1,0},{2,3},{3,2},{4,5},{5,4},{6,7},{7,6},{8,9},{9,8},{10,11... | collective-permute-start | bytes 196616 | tf_op jit(solution)/shard_map/ppermute | solution.py:398
  24.0 0.7 %copy.6 = f32[2,64,64]{2,1,0:T(8,128)} copy(f32[2,64,64]{1,2,0:T(8,128)S(1)} %slice_bitcast_fusion) | data formatting | bytes 65536
  24.7 0.2 collective-permute-done.8
  24.9 0.7 %fusion.2 = f32[4,64,128]{2,1,0:T(8,128)} fusion(f32[1,2,2,64,128]{4,3,2,1,0:T(8,128)S(1)} %fusion.1, bf16[4,64,128]{2,1,0:T(8,128)(2,1)S(1)} %collective-permute-done.8), kind=kLoop, calls=%fused_computation.6 | loop fusion | flops 98304 | bytes 327680 | tf_op jit(solution)/shard_map/mul | solution.py:399
  (7 shorter events, 0.1 us)
Async XLA Ops:
  2.5 5.5 %collective-permute-start.1 = (bf16[2,128,128]{2,1,0:T(8,128)(2,1)S(1)}, bf16[2,128,128]{2,1,0:T(8,128)(2,1)S(1)}, u32[]{:S(2)}, u32[]{:S(2)}) collective-permute-start(bf16[2,128,128]{2,1,0:T(8,128)(2,1)S(1)} %get-tuple-element.22), channel_id=1, source_target_pairs={{0,2},{2,0},{1,3},{3,1},{4,6},{6,4},{5,7},{7,5},{8,10},{10,8},{9,1... | collective-permute-start | bytes 196616 | tf_op jit(solution)/shard_map/ppermute | solution.py:277
  6.0 6.7 %copy-start = (f32[2,64,64]{2,1,0:T(8,128)S(1)}, f32[2,64,64]{2,1,0:T(8,128)}, u32[]{:S(2)}) copy-start(f32[2,64,64]{2,1,0:T(8,128)} %target.1) | copy-start | bytes 98308
  6.0 11.2 %collective-permute-start = (bf16[2,4,128,128]{3,2,1,0:T(8,128)(2,1)S(1)}, bf16[2,4,128,128]{3,2,1,0:T(8,128)(2,1)S(1)}, u32[]{:S(2)}, u32[]{:S(2)}) collective-permute-start(bf16[2,4,128,128]{3,2,1,0:T(8,128)(2,1)S(1)} %shard_map.61), channel_id=1, source_target_pairs={{0,2},{2,0},{1,3},{3,1},{4,6},{6,4},{5,7},{7,5},{8,10},{10,8},{9,1... | collective-permute-start | bytes 786440 | tf_op jit(solution)/shard_map/ppermute | solution.py:277
  8.0 6.4 %collective-permute-start.2 = (bf16[2,128,128]{2,1,0:T(8,128)(2,1)S(1)}, bf16[2,128,128]{2,1,0:T(8,128)(2,1)S(1)}, u32[]{:S(2)}, u32[]{:S(2)}) collective-permute-start(bf16[2,128,128]{2,1,0:T(8,128)(2,1)S(1)} %add_convert_fusion.refs_5_), channel_id=1, source_target_pairs={{0,12},{4,8},{8,4},{12,0},{1,13},{5,9},{9,5},{13,1},{2,14},{6,10},... | collective-permute-start | bytes 196616 | tf_op jit(solution)/shard_map/ppermute | solution.py:277
  12.0 5.2 %collective-permute-start.3 = (bf16[2,128,128]{2,1,0:T(8,128)(2,1)S(1)}, bf16[2,128,128]{2,1,0:T(8,128)(2,1)S(1)}, u32[]{:S(2)}, u32[]{:S(2)}) collective-permute-start(bf16[2,128,128]{2,1,0:T(8,128)(2,1)S(1)} %add_convert_fusion.refs_5_), channel_id=1, source_target_pairs={{0,8},{4,12},{8,0},{12,4},{1,9},{5,13},{9,1},{13,5},{2,10},{6,14},... | collective-permute-start | bytes 196616 | tf_op jit(solution)/shard_map/ppermute | solution.py:277
  12.1 5.2 %collective-permute-start.4 = (bf16[2,128,128]{2,1,0:T(8,128)(2,1)S(1)}, bf16[2,128,128]{2,1,0:T(8,128)(2,1)S(1)}, u32[]{:S(2)}, u32[]{:S(2)}) collective-permute-start(bf16[2,128,128]{2,1,0:T(8,128)(2,1)S(1)} %add_convert_fusion.refs_5_), channel_id=1, source_target_pairs={{0,4},{4,0},{8,12},{12,8},{1,5},{5,1},{9,13},{13,9},{2,6},{6,2},{1... | collective-permute-start | bytes 196616 | tf_op jit(solution)/shard_map/ppermute | solution.py:277
  18.0 5.0 %collective-permute-start.7 = (bf16[64,128]{1,0:T(8,128)(2,1)S(1)}, bf16[64,128]{1,0:T(8,128)(2,1)S(1)}, u32[]{:S(2)}, u32[]{:S(2)}) collective-permute-start(bf16[64,128]{1,0:T(8,128)(2,1)S(1)} %get-tuple-element.29), channel_id=1, source_target_pairs={{0,13},{1,12},{4,9},{5,8},{8,5},{9,4},{12,1},{13,0},{2,15},{3,14},... | collective-permute-start | bytes 49160 | tf_op jit(solution)/shard_map/ppermute | solution.py:295
  18.1 5.0 %collective-permute-start.6 = (bf16[64,128]{1,0:T(8,128)(2,1)S(1)}, bf16[64,128]{1,0:T(8,128)(2,1)S(1)}, u32[]{:S(2)}, u32[]{:S(2)}) collective-permute-start(bf16[64,128]{1,0:T(8,128)(2,1)S(1)} %get-tuple-element.30), channel_id=1, source_target_pairs={{0,8},{1,9},{4,12},{5,13},{8,0},{9,1},{12,4},{13,5},{2,10},{3,11},... | collective-permute-start | bytes 49160 | tf_op jit(solution)/shard_map/ppermute | solution.py:295
  20.1 3.2 %collective-permute-start.5 = (bf16[64,128]{1,0:T(8,128)(2,1)S(1)}, bf16[64,128]{1,0:T(8,128)(2,1)S(1)}, u32[]{:S(2)}, u32[]{:S(2)}) collective-permute-start(bf16[64,128]{1,0:T(8,128)(2,1)S(1)} %get-tuple-element.31), channel_id=1, source_target_pairs={{0,5},{1,4},{4,1},{5,0},{8,13},{9,12},{12,9},{13,8},{2,7},{3,6},{6... | collective-permute-start | bytes 49160 | tf_op jit(solution)/shard_map/ppermute | solution.py:295
  23.4 1.5 %collective-permute-start.8 = (bf16[4,64,128]{2,1,0:T(8,128)(2,1)S(1)}, bf16[4,64,128]{2,1,0:T(8,128)(2,1)S(1)}, u32[]{:S(2)}, u32[]{:S(2)}) collective-permute-start(bf16[4,64,128]{2,1,0:T(8,128)(2,1)S(1)} %bitcast_convert_fusion), channel_id=1, source_target_pairs={{0,1},{1,0},{2,3},{3,2},{4,5},{5,4},{6,7},{7,6},{8,9},{9,8},{10,11... | collective-permute-start | bytes 196616 | tf_op jit(solution)/shard_map/ppermute | solution.py:398

commit v2 on v1

--- a/solution.py
+++ b/solution.py
@@ -92,14 +92,8 @@
     row = lax.broadcasted_iota(jnp.int32, (2 * focus, polars * height), 1)
     row = block * height + lax.rem(row, height)
     inner = []
-    own = []
     for wave in range(waves):
         copies[2 * wave + 1].wait()
-        parts = []
-        for part in range(2):
-            value = kern[wave, part, tile_row].astype(jnp.float32)
-            parts.append(diagonal(one_block(value, block, side // height), polars))
-        own.append(twice(jnp.concatenate(parts, axis=0).astype(kern.dtype), 1))
         copies[2 * wave + 2].wait()
 
         def add_tile(tile, value):
@@ -115,6 +109,13 @@
 
         zero = jnp.zeros((2 * focus, polars * height), jnp.float32)
         inner.append(over_tiles(tiles, add_tile, zero))
+    own = []
+    for wave in range(waves):
+        parts = []
+        for part in range(2):
+            value = kern[wave, part, tile_row].astype(jnp.float32)
+            parts.append(diagonal(one_block(value, block, side // height), polars))
+        own.append(twice(jnp.concatenate(parts, axis=0).astype(kern.dtype), 1))
     for wave in range(waves):
         both = dot(jnp.concatenate(two_terms(inner[wave]), axis=1), own[wave], (1, 1))
         real, imag = both[:, : polars * focus], both[:, polars * focus :]

time: 25.7 us -> 25.6 us (level)
  no operation moved by 1% of the time
where the time goes in v2:
time: 25.6 us; the launch traced here: 25.5 us
  starting transfers between devices  12.2 us (48%)
  waiting for transfers between devices  5.81 us (23%)
  Pallas kernels  5.21 us (20%)
  other arithmetic  0.75 us (3%)
  local copies, waits for them, and re-layouts  0.73 us (3%)
  between operations  0.72 us (3%)
    ppermute x5, starting transfers between devices, partners(): lax.ppermute(value(d), axis, pairs(count, d))  7.76 us
    pallas_call x5, Pallas kernels, call(): pl.pallas_call(kernel, out_shape=out_shape, in_specs=[pl.BlockSpec(memory...  5.21 us
    ppermute x5, waiting for transfers between devices, partners(): lax.ppermute(value(d), axis, pairs(count, d))  4.62 us
    ppermute x3, starting transfers between devices, crosswise(): lax.ppermute(value(d), ('gx', 'wa'), routes(d))  3.89 us
    ppermute x3, waiting for transfers between devices, crosswise(): lax.ppermute(value(d), ('gx', 'wa'), routes(d))  1 us
    unnamed x3, local copies, waits for them, and re-layouts  0.72 us
    mul x1, other arithmetic, on_device(): design_grad = 0.5 * (own + other.astype(jnp.float32))  0.67 us
    ppermute x1, starting transfers between devices, on_device(): other = lax.ppermute(own.astype(jnp.bfloat16), 'wa', pairs(2, 1))  0.6 us
  transfers between devices with their start and end apart: 9, of which 6 were waited for; matrix products, arithmetic and copies ran while one was open for 3% of the time, Pallas kernels for 11%

profile of v2, /device:TPU:0, one launch (start us, length us, event | category | flops | bytes accessed | tf_op | source)
XLA Modules:
  0.0 25.5 jit_solution(6236799863418130152)
XLA Ops:
  0.6 1.7 %shard_map.59 = (bf16[2,128,128]{2,1,0:T(8,128)(2,1)S(1)}, bf16[2,2,2,4,64,128]{5,4,3,2,1,0:T(8,128)(2,1)S(1)}, bf16[2,2,4,64,128]{4,3,2,1,0:T(8,128)(2,1)S(1)}, s32[4,8,128]{2,1,0:T(8,128)S(1)}) custom-call(s32[1,4]{1,0:T(1,128)} %rows_far.1, bf16[2,2,2,1,4,64,128]{6,5,4,3,2,1,0:T(8,128)(2,1)} %field_far.1, bf16[2,2,4,64,128]{4,3,2,1,0:T(8,128)(2,1)} %kern_far.1), custom_call_target="tpu_custom_call" | custom-call | tf_op jit(solution)/shard_map/pallas_call | solution.py:263
  2.4 3.0 %collective-permute-start.1 = (bf16[2,128,128]{2,1,0:T(8,128)(2,1)S(1)}, bf16[2,128,128]{2,1,0:T(8,128)(2,1)S(1)}, u32[]{:S(2)}, u32[]{:S(2)}) collective-permute-start(bf16[2,128,128]{2,1,0:T(8,128)(2,1)S(1)} %get-tuple-element.22), channel_id=1, source_target_pairs={{0,2},{2,0},{1,3},{3,1},{4,6},{6,4},{5,7},{7,5},{8,10},{10,8},{9,1... | collective-permute-start | bytes 196616 | tf_op jit(solution)/shard_map/ppermute | solution.py:278
  5.4 0.5 %shard_map.61 = bf16[2,4,128,128]{3,2,1,0:T(8,128)(2,1)S(1)} custom-call(bf16[2,2,2,4,64,128]{5,4,3,2,1,0:T(8,128)(2,1)S(1)} %get-tuple-element.14.field, s32[4,8,128]{2,1,0:T(8,128)S(1)} %get-tuple-element.15.counts), custom_call_target="tpu_custom_call" | custom-call | tf_op jit(solution)/shard_map/pallas_call | solution.py:263
  5.9 0.0 copy-start
  5.9 0.1 collective-permute-start
  6.0 1.9 %collective-permute-done.1 = bf16[2,128,128]{2,1,0:T(8,128)(2,1)S(1)} collective-permute-done((bf16[2,128,128]{2,1,0:T(8,128)(2,1)S(1)}, bf16[2,128,128]{2,1,0:T(8,128)(2,1)S(1)}, u32[]{:S(2)}, u32[]{:S(2)}) %collective-permute-start.1) | collective-permute-done | bytes 65568 | tf_op jit(solution)/shard_map/ppermute | solution.py:278
  7.9 4.0 %collective-permute-start.2 = (bf16[2,128,128]{2,1,0:T(8,128)(2,1)S(1)}, bf16[2,128,128]{2,1,0:T(8,128)(2,1)S(1)}, u32[]{:S(2)}, u32[]{:S(2)}) collective-permute-start(bf16[2,128,128]{2,1,0:T(8,128)(2,1)S(1)} %add_convert_fusion.refs_5_), channel_id=1, source_target_pairs={{0,12},{4,8},{8,4},{12,0},{1,13},{5,9},{9,5},{13,1},{2,14},{6,10},... | collective-permute-start | bytes 196616 | tf_op jit(solution)/shard_map/ppermute | solution.py:278
  11.9 0.0 collective-permute-start.3
  11.9 0.6 %collective-permute-start.4 = (bf16[2,128,128]{2,1,0:T(8,128)(2,1)S(1)}, bf16[2,128,128]{2,1,0:T(8,128)(2,1)S(1)}, u32[]{:S(2)}, u32[]{:S(2)}) collective-permute-start(bf16[2,128,128]{2,1,0:T(8,128)(2,1)S(1)} %add_convert_fusion.refs_5_), channel_id=1, source_target_pairs={{0,4},{4,0},{8,12},{12,8},{1,5},{5,1},{9,13},{13,9},{2,6},{6,2},{1... | collective-permute-start | bytes 196616 | tf_op jit(solution)/shard_map/ppermute | solution.py:278
  12.6 0.0 copy-done
  12.6 1.8 %shard_map.60 = (f32[2,64,128]{2,1,0:T(8,128)S(1)}, bf16[2,256,256]{2,1,0:T(8,128)(2,1)S(1)}, bf16[2,4,128,256]{3,2,1,0:T(8,128)(2,1)S(1)}, bf16[2,4,128,256]{3,...) custom-call(bf16[2,2,2,4,64,128]{5,4,3,2,1,0:T(8,128)(2,1)S(1)} %get-tuple-element.14.field, ...), custom_call_target="tpu_custom_call" | custom-call | tf_op jit(solution)/shard_map/pallas_call | solution.py:263
  14.4 0.0 collective-permute-done.2.refs_2_
  14.4 2.7 %collective-permute-done.3.refs_3_ = bf16[2,128,128]{2,1,0:T(8,128)(2,1)S(1)} collective-permute-done((bf16[2,128,128]{2,1,0:T(8,128)(2,1)S(1)}, bf16[2,128,128]{2,1,0:T(8,128)(2,1)S(1)}, u32[]{:S(2)}, u32[]{:S(2)}) %collective-permute-start.3) | collective-permute-done | bytes 65568 | tf_op jit(solution)/shard_map/ppermute | solution.py:278
  17.1 0.0 collective-permute-done.4.refs_4_
  17.1 0.0 collective-permute-done.refs_1_
  17.1 0.7 %shard_map.62 = (f32[2,64,128]{2,1,0:T(8,128)S(1)}, bf16[2,256,256]{2,1,0:T(8,128)(2,1)S(1)}, bf16[4,64,128]{2,1,0:T(8,128)(2,1)S(1)}) custom-call(bf16[2,256,256]{2,1,0:T(8,128)(2,1)S(1)} %get-tuple-element.18.row_kern, bf16[2,4,128,256]{3,2,1,0:T(8,128)(2,1)S(1)} %get-tuple-element.19.turn_kern, f32[2,64,128]{2,1,0:T(8,128)S(1)} %get-tuple-element.20.goal, ...), custom_call_target="tpu_custom_call" | custom-call | tf_op jit(solution)/shard_map/pallas_call | solution.py:263
  17.9 0.1 collective-permute-start.7
  17.9 2.1 %collective-permute-start.6 = (bf16[64,128]{1,0:T(8,128)(2,1)S(1)}, bf16[64,128]{1,0:T(8,128)(2,1)S(1)}, u32[]{:S(2)}, u32[]{:S(2)}) collective-permute-start(bf16[64,128]{1,0:T(8,128)(2,1)S(1)} %get-tuple-element.30), channel_id=1, source_target_pairs={{0,8},{1,9},{4,12},{5,13},{8,0},{9,1},{12,4},{13,5},{2,10},{3,11},... | collective-permute-start | bytes 49160 | tf_op jit(solution)/shard_map/ppermute | solution.py:296
  20.0 1.7 %collective-permute-start.5 = (bf16[64,128]{1,0:T(8,128)(2,1)S(1)}, bf16[64,128]{1,0:T(8,128)(2,1)S(1)}, u32[]{:S(2)}, u32[]{:S(2)}) collective-permute-start(bf16[64,128]{1,0:T(8,128)(2,1)S(1)} %get-tuple-element.31), channel_id=1, source_target_pairs={{0,5},{1,4},{4,1},{5,0},{8,13},{9,12},{12,9},{13,8},{2,7},{3,6},{6... | collective-permute-start | bytes 49160 | tf_op jit(solution)/shard_map/ppermute | solution.py:296
  21.7 0.4 %shard_map.63 = f32[4,64,128]{2,1,0:T(8,128)S(1)} custom-call(bf16[2,2,2,4,64,128]{5,4,3,2,1,0:T(8,128)(2,1)S(1)} %get-tuple-element.14.field, s32[4,8,128]{2,1,0:T(8,128)S(1)} %get-tuple-element.15.counts, bf16[2,4,128,256]{3,2,1,0:T(8,128)(2,1)S(1)} %get-tuple-element.17.both_kern, bf16[2,256,256]{2,1,0:T(8,128)(2,1)S(1)} %get-tuple-element.23.near), custom_call_target="tpu_custom_call" | custom-call | tf_op jit(solution)/shard_map/pallas_call | solution.py:263
  22.2 0.7 %collective-permute-done.7 = bf16[64,128]{1,0:T(8,128)(2,1)S(1)} collective-permute-done((bf16[64,128]{1,0:T(8,128)(2,1)S(1)}, bf16[64,128]{1,0:T(8,128)(2,1)S(1)}, u32[]{:S(2)}, u32[]{:S(2)}) %collective-permute-start.7) | collective-permute-done | bytes 16416 | tf_op jit(solution)/shard_map/ppermute | solution.py:296
  22.9 0.1 collective-permute-done.6
  23.0 0.2 collective-permute-done.5
  23.3 0.6 %collective-permute-start.8 = (bf16[4,64,128]{2,1,0:T(8,128)(2,1)S(1)}, bf16[4,64,128]{2,1,0:T(8,128)(2,1)S(1)}, u32[]{:S(2)}, u32[]{:S(2)}) collective-permute-start(bf16[4,64,128]{2,1,0:T(8,128)(2,1)S(1)} %bitcast_convert_fusion), channel_id=1, source_target_pairs={{0,1},{1,0},{2,3},{3,2},{4,5},{5,4},{6,7},{7,6},{8,9},{9,8},{10,11... | collective-permute-start | bytes 196616 | tf_op jit(solution)/shard_map/ppermute | solution.py:399
  23.9 0.7 %copy.6 = f32[2,64,64]{2,1,0:T(8,128)} copy(f32[2,64,64]{1,2,0:T(8,128)S(1)} %slice_bitcast_fusion) | data formatting | bytes 65536
  24.6 0.2 collective-permute-done.8
  24.8 0.7 %fusion.2 = f32[4,64,128]{2,1,0:T(8,128)} fusion(f32[1,2,2,64,128]{4,3,2,1,0:T(8,128)S(1)} %fusion.1, bf16[4,64,128]{2,1,0:T(8,128)(2,1)S(1)} %collective-permute-done.8), kind=kLoop, calls=%fused_computation.6 | loop fusion | flops 98304 | bytes 327680 | tf_op jit(solution)/shard_map/mul | solution.py:400
  (7 shorter events, 0.1 us)
Async XLA Ops:
  2.4 5.5 %collective-permute-start.1 = (bf16[2,128,128]{2,1,0:T(8,128)(2,1)S(1)}, bf16[2,128,128]{2,1,0:T(8,128)(2,1)S(1)}, u32[]{:S(2)}, u32[]{:S(2)}) collective-permute-start(bf16[2,128,128]{2,1,0:T(8,128)(2,1)S(1)} %get-tuple-element.22), channel_id=1, source_target_pairs={{0,2},{2,0},{1,3},{3,1},{4,6},{6,4},{5,7},{7,5},{8,10},{10,8},{9,1... | collective-permute-start | bytes 196616 | tf_op jit(solution)/shard_map/ppermute | solution.py:278
  5.9 6.7 %copy-start = (f32[2,64,64]{2,1,0:T(8,128)S(1)}, f32[2,64,64]{2,1,0:T(8,128)}, u32[]{:S(2)}) copy-start(f32[2,64,64]{2,1,0:T(8,128)} %target.1) | copy-start | bytes 98308
  5.9 11.2 %collective-permute-start = (bf16[2,4,128,128]{3,2,1,0:T(8,128)(2,1)S(1)}, bf16[2,4,128,128]{3,2,1,0:T(8,128)(2,1)S(1)}, u32[]{:S(2)}, u32[]{:S(2)}) collective-permute-start(bf16[2,4,128,128]{3,2,1,0:T(8,128)(2,1)S(1)} %shard_map.61), channel_id=1, source_target_pairs={{0,2},{2,0},{1,3},{3,1},{4,6},{6,4},{5,7},{7,5},{8,10},{10,8},{9,1... | collective-permute-start | bytes 786440 | tf_op jit(solution)/shard_map/ppermute | solution.py:278
  7.9 6.4 %collective-permute-start.2 = (bf16[2,128,128]{2,1,0:T(8,128)(2,1)S(1)}, bf16[2,128,128]{2,1,0:T(8,128)(2,1)S(1)}, u32[]{:S(2)}, u32[]{:S(2)}) collective-permute-start(bf16[2,128,128]{2,1,0:T(8,128)(2,1)S(1)} %add_convert_fusion.refs_5_), channel_id=1, source_target_pairs={{0,12},{4,8},{8,4},{12,0},{1,13},{5,9},{9,5},{13,1},{2,14},{6,10},... | collective-permute-start | bytes 196616 | tf_op jit(solution)/shard_map/ppermute | solution.py:278
  11.9 5.2 %collective-permute-start.3 = (bf16[2,128,128]{2,1,0:T(8,128)(2,1)S(1)}, bf16[2,128,128]{2,1,0:T(8,128)(2,1)S(1)}, u32[]{:S(2)}, u32[]{:S(2)}) collective-permute-start(bf16[2,128,128]{2,1,0:T(8,128)(2,1)S(1)} %add_convert_fusion.refs_5_), channel_id=1, source_target_pairs={{0,8},{4,12},{8,0},{12,4},{1,9},{5,13},{9,1},{13,5},{2,10},{6,14},... | collective-permute-start | bytes 196616 | tf_op jit(solution)/shard_map/ppermute | solution.py:278
  11.9 5.2 %collective-permute-start.4 = (bf16[2,128,128]{2,1,0:T(8,128)(2,1)S(1)}, bf16[2,128,128]{2,1,0:T(8,128)(2,1)S(1)}, u32[]{:S(2)}, u32[]{:S(2)}) collective-permute-start(bf16[2,128,128]{2,1,0:T(8,128)(2,1)S(1)} %add_convert_fusion.refs_5_), channel_id=1, source_target_pairs={{0,4},{4,0},{8,12},{12,8},{1,5},{5,1},{9,13},{13,9},{2,6},{6,2},{1... | collective-permute-start | bytes 196616 | tf_op jit(solution)/shard_map/ppermute | solution.py:278
  17.9 5.0 %collective-permute-start.7 = (bf16[64,128]{1,0:T(8,128)(2,1)S(1)}, bf16[64,128]{1,0:T(8,128)(2,1)S(1)}, u32[]{:S(2)}, u32[]{:S(2)}) collective-permute-start(bf16[64,128]{1,0:T(8,128)(2,1)S(1)} %get-tuple-element.29), channel_id=1, source_target_pairs={{0,13},{1,12},{4,9},{5,8},{8,5},{9,4},{12,1},{13,0},{2,15},{3,14},... | collective-permute-start | bytes 49160 | tf_op jit(solution)/shard_map/ppermute | solution.py:296
  17.9 5.0 %collective-permute-start.6 = (bf16[64,128]{1,0:T(8,128)(2,1)S(1)}, bf16[64,128]{1,0:T(8,128)(2,1)S(1)}, u32[]{:S(2)}, u32[]{:S(2)}) collective-permute-start(bf16[64,128]{1,0:T(8,128)(2,1)S(1)} %get-tuple-element.30), channel_id=1, source_target_pairs={{0,8},{1,9},{4,12},{5,13},{8,0},{9,1},{12,4},{13,5},{2,10},{3,11},... | collective-permute-start | bytes 49160 | tf_op jit(solution)/shard_map/ppermute | solution.py:296
  20.0 3.2 %collective-permute-start.5 = (bf16[64,128]{1,0:T(8,128)(2,1)S(1)}, bf16[64,128]{1,0:T(8,128)(2,1)S(1)}, u32[]{:S(2)}, u32[]{:S(2)}) collective-permute-start(bf16[64,128]{1,0:T(8,128)(2,1)S(1)} %get-tuple-element.31), channel_id=1, source_target_pairs={{0,5},{1,4},{4,1},{5,0},{8,13},{9,12},{12,9},{13,8},{2,7},{3,6},{6... | collective-permute-start | bytes 49160 | tf_op jit(solution)/shard_map/ppermute | solution.py:296
  23.3 1.5 %collective-permute-start.8 = (bf16[4,64,128]{2,1,0:T(8,128)(2,1)S(1)}, bf16[4,64,128]{2,1,0:T(8,128)(2,1)S(1)}, u32[]{:S(2)}, u32[]{:S(2)}) collective-permute-start(bf16[4,64,128]{2,1,0:T(8,128)(2,1)S(1)} %bitcast_convert_fusion), channel_id=1, source_target_pairs={{0,1},{1,0},{2,3},{3,2},{4,5},{5,4},{6,7},{7,6},{8,9},{9,8},{10,11... | collective-permute-start | bytes 196616 | tf_op jit(solution)/shard_map/ppermute | solution.py:399

commit v3 on v2

--- a/solution.py
+++ b/solution.py
@@ -91,10 +91,10 @@
     over_tiles(tiles, put_count, 0)
     row = lax.broadcasted_iota(jnp.int32, (2 * focus, polars * height), 1)
     row = block * height + lax.rem(row, height)
+    for copy in copies[1:]:
+        copy.wait()
     inner = []
     for wave in range(waves):
-        copies[2 * wave + 1].wait()
-        copies[2 * wave + 2].wait()
 
         def add_tile(tile, value):
             planes = [field[wave, :, part, tile] for part in range(2)]

time: 25.6 us -> 25.5 us (level)
  no operation moved by 1% of the time
where the time goes in v3:
time: 25.5 us; the launch traced here: 25.4 us
  starting transfers between devices  12.3 us (48%)
  waiting for transfers between devices  5.81 us (23%)
  Pallas kernels  5.13 us (20%)
  other arithmetic  0.75 us (3%)
  local copies, waits for them, and re-layouts  0.73 us (3%)
  between operations  0.72 us (3%)
    ppermute x5, starting transfers between devices, partners(): lax.ppermute(value(d), axis, pairs(count, d))  7.78 us
    pallas_call x5, Pallas kernels, call(): pl.pallas_call(kernel, out_shape=out_shape, in_specs=[pl.BlockSpec(memory...  5.13 us
    ppermute x5, waiting for transfers between devices, partners(): lax.ppermute(value(d), axis, pairs(count, d))  4.62 us
    ppermute x3, starting transfers between devices, crosswise(): lax.ppermute(value(d), ('gx', 'wa'), routes(d))  3.89 us
    ppermute x3, waiting for transfers between devices, crosswise(): lax.ppermute(value(d), ('gx', 'wa'), routes(d))  1 us
    unnamed x3, local copies, waits for them, and re-layouts  0.72 us
    mul x1, other arithmetic, on_device(): design_grad = 0.5 * (own + other.astype(jnp.float32))  0.67 us
    ppermute x1, starting transfers between devices, on_device(): other = lax.ppermute(own.astype(jnp.bfloat16), 'wa', pairs(2, 1))  0.6 us
  transfers between devices with their start and end apart: 9, of which 6 were waited for; matrix products, arithmetic and copies ran while one was open for 3% of the time, Pallas kernels for 11%

profile of v3, /device:TPU:0, one launch (start us, length us, event | category | flops | bytes accessed | tf_op | source)
XLA Modules:
  0.0 25.4 jit_solution(16488491957386331963)
XLA Ops:
  0.6 1.7 %shard_map.59 = (bf16[2,128,128]{2,1,0:T(8,128)(2,1)S(1)}, bf16[2,2,2,4,64,128]{5,4,3,2,1,0:T(8,128)(2,1)S(1)}, bf16[2,2,4,64,128]{4,3,2,1,0:T(8,128)(2,1)S(1)}, s32[4,8,128]{2,1,0:T(8,128)S(1)}) custom-call(s32[1,4]{1,0:T(1,128)} %rows_far.1, bf16[2,2,2,1,4,64,128]{6,5,4,3,2,1,0:T(8,128)(2,1)} %field_far.1, bf16[2,2,4,64,128]{4,3,2,1,0:T(8,128)(2,1)} %kern_far.1), custom_call_target="tpu_custom_call" | custom-call | tf_op jit(solution)/shard_map/pallas_call | solution.py:263
  2.3 3.0 %collective-permute-start.1 = (bf16[2,128,128]{2,1,0:T(8,128)(2,1)S(1)}, bf16[2,128,128]{2,1,0:T(8,128)(2,1)S(1)}, u32[]{:S(2)}, u32[]{:S(2)}) collective-permute-start(bf16[2,128,128]{2,1,0:T(8,128)(2,1)S(1)} %get-tuple-element.22), channel_id=1, source_target_pairs={{0,2},{2,0},{1,3},{3,1},{4,6},{6,4},{5,7},{7,5},{8,10},{10,8},{9,1... | collective-permute-start | bytes 196616 | tf_op jit(solution)/shard_map/ppermute | solution.py:278
  5.3 0.5 %shard_map.61 = bf16[2,4,128,128]{3,2,1,0:T(8,128)(2,1)S(1)} custom-call(bf16[2,2,2,4,64,128]{5,4,3,2,1,0:T(8,128)(2,1)S(1)} %get-tuple-element.14.field, s32[4,8,128]{2,1,0:T(8,128)S(1)} %get-tuple-element.15.counts), custom_call_target="tpu_custom_call" | custom-call | tf_op jit(solution)/shard_map/pallas_call | solution.py:263
  5.8 0.0 copy-start
  5.8 0.1 collective-permute-start
  5.9 1.9 %collective-permute-done.1 = bf16[2,128,128]{2,1,0:T(8,128)(2,1)S(1)} collective-permute-done((bf16[2,128,128]{2,1,0:T(8,128)(2,1)S(1)}, bf16[2,128,128]{2,1,0:T(8,128)(2,1)S(1)}, u32[]{:S(2)}, u32[]{:S(2)}) %collective-permute-start.1) | collective-permute-done | bytes 65568 | tf_op jit(solution)/shard_map/ppermute | solution.py:278
  7.8 4.0 %collective-permute-start.2 = (bf16[2,128,128]{2,1,0:T(8,128)(2,1)S(1)}, bf16[2,128,128]{2,1,0:T(8,128)(2,1)S(1)}, u32[]{:S(2)}, u32[]{:S(2)}) collective-permute-start(bf16[2,128,128]{2,1,0:T(8,128)(2,1)S(1)} %add_convert_fusion.refs_5_), channel_id=1, source_target_pairs={{0,12},{4,8},{8,4},{12,0},{1,13},{5,9},{9,5},{13,1},{2,14},{6,10},... | collective-permute-start | bytes 196616 | tf_op jit(solution)/shard_map/ppermute | solution.py:278
  11.9 0.0 collective-permute-start.3
  11.9 0.6 %collective-permute-start.4 = (bf16[2,128,128]{2,1,0:T(8,128)(2,1)S(1)}, bf16[2,128,128]{2,1,0:T(8,128)(2,1)S(1)}, u32[]{:S(2)}, u32[]{:S(2)}) collective-permute-start(bf16[2,128,128]{2,1,0:T(8,128)(2,1)S(1)} %add_convert_fusion.refs_5_), channel_id=1, source_target_pairs={{0,4},{4,0},{8,12},{12,8},{1,5},{5,1},{9,13},{13,9},{2,6},{6,2},{1... | collective-permute-start | bytes 196616 | tf_op jit(solution)/shard_map/ppermute | solution.py:278
  12.5 0.0 copy-done
  12.5 1.8 %shard_map.60 = (f32[2,64,128]{2,1,0:T(8,128)S(1)}, bf16[2,256,256]{2,1,0:T(8,128)(2,1)S(1)}, bf16[2,4,128,256]{3,2,1,0:T(8,128)(2,1)S(1)}, bf16[2,4,128,256]{3,...) custom-call(bf16[2,2,2,4,64,128]{5,4,3,2,1,0:T(8,128)(2,1)S(1)} %get-tuple-element.14.field, ...), custom_call_target="tpu_custom_call" | custom-call | tf_op jit(solution)/shard_map/pallas_call | solution.py:263
  14.3 0.0 collective-permute-done.2.refs_2_
  14.3 2.7 %collective-permute-done.3.refs_3_ = bf16[2,128,128]{2,1,0:T(8,128)(2,1)S(1)} collective-permute-done((bf16[2,128,128]{2,1,0:T(8,128)(2,1)S(1)}, bf16[2,128,128]{2,1,0:T(8,128)(2,1)S(1)}, u32[]{:S(2)}, u32[]{:S(2)}) %collective-permute-start.3) | collective-permute-done | bytes 65568 | tf_op jit(solution)/shard_map/ppermute | solution.py:278
  17.0 0.0 collective-permute-done.4.refs_4_
  17.0 0.0 collective-permute-done.refs_1_
  17.0 0.7 %shard_map.62 = (f32[2,64,128]{2,1,0:T(8,128)S(1)}, bf16[2,256,256]{2,1,0:T(8,128)(2,1)S(1)}, bf16[4,64,128]{2,1,0:T(8,128)(2,1)S(1)}) custom-call(bf16[2,256,256]{2,1,0:T(8,128)(2,1)S(1)} %get-tuple-element.18.row_kern, bf16[2,4,128,256]{3,2,1,0:T(8,128)(2,1)S(1)} %get-tuple-element.19.turn_kern, f32[2,64,128]{2,1,0:T(8,128)S(1)} %get-tuple-element.20.goal, ...), custom_call_target="tpu_custom_call" | custom-call | tf_op jit(solution)/shard_map/pallas_call | solution.py:263
  17.8 0.1 collective-permute-start.7
  17.9 2.1 %collective-permute-start.6 = (bf16[64,128]{1,0:T(8,128)(2,1)S(1)}, bf16[64,128]{1,0:T(8,128)(2,1)S(1)}, u32[]{:S(2)}, u32[]{:S(2)}) collective-permute-start(bf16[64,128]{1,0:T(8,128)(2,1)S(1)} %get-tuple-element.30), channel_id=1, source_target_pairs={{0,8},{1,9},{4,12},{5,13},{8,0},{9,1},{12,4},{13,5},{2,10},{3,11},... | collective-permute-start | bytes 49160 | tf_op jit(solution)/shard_map/ppermute | solution.py:296
  20.0 1.7 %collective-permute-start.5 = (bf16[64,128]{1,0:T(8,128)(2,1)S(1)}, bf16[64,128]{1,0:T(8,128)(2,1)S(1)}, u32[]{:S(2)}, u32[]{:S(2)}) collective-permute-start(bf16[64,128]{1,0:T(8,128)(2,1)S(1)} %get-tuple-element.31), channel_id=1, source_target_pairs={{0,5},{1,4},{4,1},{5,0},{8,13},{9,12},{12,9},{13,8},{2,7},{3,6},{6... | collective-permute-start | bytes 49160 | tf_op jit(solution)/shard_map/ppermute | solution.py:296
  21.7 0.4 %shard_map.63 = f32[4,64,128]{2,1,0:T(8,128)S(1)} custom-call(bf16[2,2,2,4,64,128]{5,4,3,2,1,0:T(8,128)(2,1)S(1)} %get-tuple-element.14.field, s32[4,8,128]{2,1,0:T(8,128)S(1)} %get-tuple-element.15.counts, bf16[2,4,128,256]{3,2,1,0:T(8,128)(2,1)S(1)} %get-tuple-element.17.both_kern, bf16[2,256,256]{2,1,0:T(8,128)(2,1)S(1)} %get-tuple-element.23.near), custom_call_target="tpu_custom_call" | custom-call | tf_op jit(solution)/shard_map/pallas_call | solution.py:263
  22.1 0.7 %collective-permute-done.7 = bf16[64,128]{1,0:T(8,128)(2,1)S(1)} collective-permute-done((bf16[64,128]{1,0:T(8,128)(2,1)S(1)}, bf16[64,128]{1,0:T(8,128)(2,1)S(1)}, u32[]{:S(2)}, u32[]{:S(2)}) %collective-permute-start.7) | collective-permute-done | bytes 16416 | tf_op jit(solution)/shard_map/ppermute | solution.py:296
  22.8 0.1 collective-permute-done.6
  22.9 0.2 collective-permute-done.5
  23.2 0.6 %collective-permute-start.8 = (bf16[4,64,128]{2,1,0:T(8,128)(2,1)S(1)}, bf16[4,64,128]{2,1,0:T(8,128)(2,1)S(1)}, u32[]{:S(2)}, u32[]{:S(2)}) collective-permute-start(bf16[4,64,128]{2,1,0:T(8,128)(2,1)S(1)} %bitcast_convert_fusion), channel_id=1, source_target_pairs={{0,1},{1,0},{2,3},{3,2},{4,5},{5,4},{6,7},{7,6},{8,9},{9,8},{10,11... | collective-permute-start | bytes 196616 | tf_op jit(solution)/shard_map/ppermute | solution.py:399
  23.8 0.7 %copy.6 = f32[2,64,64]{2,1,0:T(8,128)} copy(f32[2,64,64]{1,2,0:T(8,128)S(1)} %slice_bitcast_fusion) | data formatting | bytes 65536
  24.5 0.2 collective-permute-done.8
  24.7 0.7 %fusion.2 = f32[4,64,128]{2,1,0:T(8,128)} fusion(f32[1,2,2,64,128]{4,3,2,1,0:T(8,128)S(1)} %fusion.1, bf16[4,64,128]{2,1,0:T(8,128)(2,1)S(1)} %collective-permute-done.8), kind=kLoop, calls=%fused_computation.6 | loop fusion | flops 98304 | bytes 327680 | tf_op jit(solution)/shard_map/mul | solution.py:400
  (7 shorter events, 0.1 us)
Async XLA Ops:
  2.3 5.5 %collective-permute-start.1 = (bf16[2,128,128]{2,1,0:T(8,128)(2,1)S(1)}, bf16[2,128,128]{2,1,0:T(8,128)(2,1)S(1)}, u32[]{:S(2)}, u32[]{:S(2)}) collective-permute-start(bf16[2,128,128]{2,1,0:T(8,128)(2,1)S(1)} %get-tuple-element.22), channel_id=1, source_target_pairs={{0,2},{2,0},{1,3},{3,1},{4,6},{6,4},{5,7},{7,5},{8,10},{10,8},{9,1... | collective-permute-start | bytes 196616 | tf_op jit(solution)/shard_map/ppermute | solution.py:278
  5.8 6.7 %copy-start = (f32[2,64,64]{2,1,0:T(8,128)S(1)}, f32[2,64,64]{2,1,0:T(8,128)}, u32[]{:S(2)}) copy-start(f32[2,64,64]{2,1,0:T(8,128)} %target.1) | copy-start | bytes 98308
  5.8 11.2 %collective-permute-start = (bf16[2,4,128,128]{3,2,1,0:T(8,128)(2,1)S(1)}, bf16[2,4,128,128]{3,2,1,0:T(8,128)(2,1)S(1)}, u32[]{:S(2)}, u32[]{:S(2)}) collective-permute-start(bf16[2,4,128,128]{3,2,1,0:T(8,128)(2,1)S(1)} %shard_map.61), channel_id=1, source_target_pairs={{0,2},{2,0},{1,3},{3,1},{4,6},{6,4},{5,7},{7,5},{8,10},{10,8},{9,1... | collective-permute-start | bytes 786440 | tf_op jit(solution)/shard_map/ppermute | solution.py:278
  7.8 6.5 %collective-permute-start.2 = (bf16[2,128,128]{2,1,0:T(8,128)(2,1)S(1)}, bf16[2,128,128]{2,1,0:T(8,128)(2,1)S(1)}, u32[]{:S(2)}, u32[]{:S(2)}) collective-permute-start(bf16[2,128,128]{2,1,0:T(8,128)(2,1)S(1)} %add_convert_fusion.refs_5_), channel_id=1, source_target_pairs={{0,12},{4,8},{8,4},{12,0},{1,13},{5,9},{9,5},{13,1},{2,14},{6,10},... | collective-permute-start | bytes 196616 | tf_op jit(solution)/shard_map/ppermute | solution.py:278
  11.9 5.2 %collective-permute-start.3 = (bf16[2,128,128]{2,1,0:T(8,128)(2,1)S(1)}, bf16[2,128,128]{2,1,0:T(8,128)(2,1)S(1)}, u32[]{:S(2)}, u32[]{:S(2)}) collective-permute-start(bf16[2,128,128]{2,1,0:T(8,128)(2,1)S(1)} %add_convert_fusion.refs_5_), channel_id=1, source_target_pairs={{0,8},{4,12},{8,0},{12,4},{1,9},{5,13},{9,1},{13,5},{2,10},{6,14},... | collective-permute-start | bytes 196616 | tf_op jit(solution)/shard_map/ppermute | solution.py:278
  11.9 5.2 %collective-permute-start.4 = (bf16[2,128,128]{2,1,0:T(8,128)(2,1)S(1)}, bf16[2,128,128]{2,1,0:T(8,128)(2,1)S(1)}, u32[]{:S(2)}, u32[]{:S(2)}) collective-permute-start(bf16[2,128,128]{2,1,0:T(8,128)(2,1)S(1)} %add_convert_fusion.refs_5_), channel_id=1, source_target_pairs={{0,4},{4,0},{8,12},{12,8},{1,5},{5,1},{9,13},{13,9},{2,6},{6,2},{1... | collective-permute-start | bytes 196616 | tf_op jit(solution)/shard_map/ppermute | solution.py:278
  17.8 5.0 %collective-permute-start.7 = (bf16[64,128]{1,0:T(8,128)(2,1)S(1)}, bf16[64,128]{1,0:T(8,128)(2,1)S(1)}, u32[]{:S(2)}, u32[]{:S(2)}) collective-permute-start(bf16[64,128]{1,0:T(8,128)(2,1)S(1)} %get-tuple-element.29), channel_id=1, source_target_pairs={{0,13},{1,12},{4,9},{5,8},{8,5},{9,4},{12,1},{13,0},{2,15},{3,14},... | collective-permute-start | bytes 49160 | tf_op jit(solution)/shard_map/ppermute | solution.py:296
  17.9 5.0 %collective-permute-start.6 = (bf16[64,128]{1,0:T(8,128)(2,1)S(1)}, bf16[64,128]{1,0:T(8,128)(2,1)S(1)}, u32[]{:S(2)}, u32[]{:S(2)}) collective-permute-start(bf16[64,128]{1,0:T(8,128)(2,1)S(1)} %get-tuple-element.30), channel_id=1, source_target_pairs={{0,8},{1,9},{4,12},{5,13},{8,0},{9,1},{12,4},{13,5},{2,10},{3,11},... | collective-permute-start | bytes 49160 | tf_op jit(solution)/shard_map/ppermute | solution.py:296
  20.0 3.2 %collective-permute-start.5 = (bf16[64,128]{1,0:T(8,128)(2,1)S(1)}, bf16[64,128]{1,0:T(8,128)(2,1)S(1)}, u32[]{:S(2)}, u32[]{:S(2)}) collective-permute-start(bf16[64,128]{1,0:T(8,128)(2,1)S(1)} %get-tuple-element.31), channel_id=1, source_target_pairs={{0,5},{1,4},{4,1},{5,0},{8,13},{9,12},{12,9},{13,8},{2,7},{3,6},{6... | collective-permute-start | bytes 49160 | tf_op jit(solution)/shard_map/ppermute | solution.py:296
  23.2 1.5 %collective-permute-start.8 = (bf16[4,64,128]{2,1,0:T(8,128)(2,1)S(1)}, bf16[4,64,128]{2,1,0:T(8,128)(2,1)S(1)}, u32[]{:S(2)}, u32[]{:S(2)}) collective-permute-start(bf16[4,64,128]{2,1,0:T(8,128)(2,1)S(1)} %bitcast_convert_fusion), channel_id=1, source_target_pairs={{0,1},{1,0},{2,3},{3,2},{4,5},{5,4},{6,7},{7,6},{8,9},{9,8},{10,11... | collective-permute-start | bytes 196616 | tf_op jit(solution)/shard_map/ppermute | solution.py:399

commit v4 on v3

--- a/solution.py
+++ b/solution.py
@@ -68,14 +68,11 @@
 def share_kernel(rows_far, field_far, kern_far, share, field, kern, counts, rows, arrived):
     waves, polars, _, tiles, height, side = field.shape
     focus = kern.shape[3]
-    copies = [pltpu.make_async_copy(rows_far, rows, arrived.at[2 * waves])]
-    for wave in range(waves):
-        copies += [
-            pltpu.make_async_copy(kern_far.at[wave], kern.at[wave], arrived.at[2 * wave]),
-            pltpu.make_async_copy(
-                field_far.at[wave, :, :, 0], field.at[wave], arrived.at[2 * wave + 1]
-            ),
-        ]
+    copies = [
+        pltpu.make_async_copy(rows_far, rows, arrived.at[0]),
+        pltpu.make_async_copy(kern_far, kern, arrived.at[1]),
+        pltpu.make_async_copy(field_far.at[:, :, :, 0], field, arrived.at[2]),
+    ]
     for copy in copies:
         copy.start()
     tile_row = lax.axis_index("gx")
@@ -340,7 +337,7 @@
             ],
             [
                 pltpu.VMEM(active_rows.shape, jnp.int32),
-                pltpu.SemaphoreType.DMA((2 * waves + 1,)),
+                pltpu.SemaphoreType.DMA((3,)),
             ],
             [
                 pltpu.with_memory_space_constraint(operand, pltpu.HBM)

time: 25.5 us -> 25.5 us (level)
  no operation moved by 1% of the time
where the time goes in v4:
time: 25.5 us; the launch traced here: 25.3 us
  starting transfers between devices  12.2 us (48%)
  waiting for transfers between devices  5.8 us (23%)
  Pallas kernels  5.09 us (20%)
  other arithmetic  0.75 us (3%)
  local copies, waits for them, and re-layouts  0.73 us (3%)
  between operations  0.72 us (3%)
    ppermute x5, starting transfers between devices, partners(): lax.ppermute(value(d), axis, pairs(count, d))  7.73 us
    pallas_call x5, Pallas kernels, call(): pl.pallas_call(kernel, out_shape=out_shape, in_specs=[pl.BlockSpec(memory...  5.09 us
    ppermute x5, waiting for transfers between devices, partners(): lax.ppermute(value(d), axis, pairs(count, d))  4.62 us
    ppermute x3, starting transfers between devices, crosswise(): lax.ppermute(value(d), ('gx', 'wa'), routes(d))  3.89 us
    ppermute x3, waiting for transfers between devices, crosswise(): lax.ppermute(value(d), ('gx', 'wa'), routes(d))  1 us
    unnamed x3, local copies, waits for them, and re-layouts  0.72 us
    mul x1, other arithmetic, on_device(): design_grad = 0.5 * (own + other.astype(jnp.float32))  0.67 us
    ppermute x1, starting transfers between devices, on_device(): other = lax.ppermute(own.astype(jnp.bfloat16), 'wa', pairs(2, 1))  0.6 us
  transfers between devices with their start and end apart: 9, of which 6 were waited for; matrix products, arithmetic and copies ran while one was open for 3% of the time, Pallas kernels for 11%

profile of v4, /device:TPU:0, one launch (start us, length us, event | category | flops | bytes accessed | tf_op | source)
XLA Modules:
  0.0 25.3 jit_solution(3321507239333580588)
XLA Ops:
  0.6 1.6 %shard_map.59 = (bf16[2,128,128]{2,1,0:T(8,128)(2,1)S(1)}, bf16[2,2,2,4,64,128]{5,4,3,2,1,0:T(8,128)(2,1)S(1)}, bf16[2,2,4,64,128]{4,3,2,1,0:T(8,128)(2,1)S(1)}, s32[4,8,128]{2,1,0:T(8,128)S(1)}) custom-call(s32[1,4]{1,0:T(1,128)} %rows_far.1, bf16[2,2,2,1,4,64,128]{6,5,4,3,2,1,0:T(8,128)(2,1)} %field_far.1, bf16[2,2,4,64,128]{4,3,2,1,0:T(8,128)(2,1)} %kern_far.1), custom_call_target="tpu_custom_call" | custom-call | tf_op jit(solution)/shard_map/pallas_call | solution.py:260
  2.3 3.0 %collective-permute-start.1 = (bf16[2,128,128]{2,1,0:T(8,128)(2,1)S(1)}, bf16[2,128,128]{2,1,0:T(8,128)(2,1)S(1)}, u32[]{:S(2)}, u32[]{:S(2)}) collective-permute-start(bf16[2,128,128]{2,1,0:T(8,128)(2,1)S(1)} %get-tuple-element.22), channel_id=1, source_target_pairs={{0,2},{2,0},{1,3},{3,1},{4,6},{6,4},{5,7},{7,5},{8,10},{10,8},{9,1... | collective-permute-start | bytes 196616 | tf_op jit(solution)/shard_map/ppermute | solution.py:275
  5.2 0.5 %shard_map.61 = bf16[2,4,128,128]{3,2,1,0:T(8,128)(2,1)S(1)} custom-call(bf16[2,2,2,4,64,128]{5,4,3,2,1,0:T(8,128)(2,1)S(1)} %get-tuple-element.14.field, s32[4,8,128]{2,1,0:T(8,128)S(1)} %get-tuple-element.15.counts), custom_call_target="tpu_custom_call" | custom-call | tf_op jit(solution)/shard_map/pallas_call | solution.py:260
  5.8 0.0 copy-start
  5.8 0.1 collective-permute-start
  5.9 1.9 %collective-permute-done.1 = bf16[2,128,128]{2,1,0:T(8,128)(2,1)S(1)} collective-permute-done((bf16[2,128,128]{2,1,0:T(8,128)(2,1)S(1)}, bf16[2,128,128]{2,1,0:T(8,128)(2,1)S(1)}, u32[]{:S(2)}, u32[]{:S(2)}) %collective-permute-start.1) | collective-permute-done | bytes 65568 | tf_op jit(solution)/shard_map/ppermute | solution.py:275
  7.8 4.0 %collective-permute-start.2 = (bf16[2,128,128]{2,1,0:T(8,128)(2,1)S(1)}, bf16[2,128,128]{2,1,0:T(8,128)(2,1)S(1)}, u32[]{:S(2)}, u32[]{:S(2)}) collective-permute-start(bf16[2,128,128]{2,1,0:T(8,128)(2,1)S(1)} %add_convert_fusion.refs_5_), channel_id=1, source_target_pairs={{0,12},{4,8},{8,4},{12,0},{1,13},{5,9},{9,5},{13,1},{2,14},{6,10},... | collective-permute-start | bytes 196616 | tf_op jit(solution)/shard_map/ppermute | solution.py:275
  11.8 0.0 collective-permute-start.3
  11.8 0.6 %collective-permute-start.4 = (bf16[2,128,128]{2,1,0:T(8,128)(2,1)S(1)}, bf16[2,128,128]{2,1,0:T(8,128)(2,1)S(1)}, u32[]{:S(2)}, u32[]{:S(2)}) collective-permute-start(bf16[2,128,128]{2,1,0:T(8,128)(2,1)S(1)} %add_convert_fusion.refs_5_), channel_id=1, source_target_pairs={{0,4},{4,0},{8,12},{12,8},{1,5},{5,1},{9,13},{13,9},{2,6},{6,2},{1... | collective-permute-start | bytes 196616 | tf_op jit(solution)/shard_map/ppermute | solution.py:275
  12.4 0.0 copy-done
  12.4 1.8 %shard_map.60 = (f32[2,64,128]{2,1,0:T(8,128)S(1)}, bf16[2,256,256]{2,1,0:T(8,128)(2,1)S(1)}, bf16[2,4,128,256]{3,2,1,0:T(8,128)(2,1)S(1)}, bf16[2,4,128,256]{3,...) custom-call(bf16[2,2,2,4,64,128]{5,4,3,2,1,0:T(8,128)(2,1)S(1)} %get-tuple-element.14.field, ...), custom_call_target="tpu_custom_call" | custom-call | tf_op jit(solution)/shard_map/pallas_call | solution.py:260
  14.2 0.0 collective-permute-done.2.refs_2_
  14.2 2.7 %collective-permute-done.3.refs_3_ = bf16[2,128,128]{2,1,0:T(8,128)(2,1)S(1)} collective-permute-done((bf16[2,128,128]{2,1,0:T(8,128)(2,1)S(1)}, bf16[2,128,128]{2,1,0:T(8,128)(2,1)S(1)}, u32[]{:S(2)}, u32[]{:S(2)}) %collective-permute-start.3) | collective-permute-done | bytes 65568 | tf_op jit(solution)/shard_map/ppermute | solution.py:275
  17.0 0.0 collective-permute-done.4.refs_4_
  17.0 0.0 collective-permute-done.refs_1_
  17.0 0.7 %shard_map.62 = (f32[2,64,128]{2,1,0:T(8,128)S(1)}, bf16[2,256,256]{2,1,0:T(8,128)(2,1)S(1)}, bf16[4,64,128]{2,1,0:T(8,128)(2,1)S(1)}) custom-call(bf16[2,256,256]{2,1,0:T(8,128)(2,1)S(1)} %get-tuple-element.18.row_kern, bf16[2,4,128,256]{3,2,1,0:T(8,128)(2,1)S(1)} %get-tuple-element.19.turn_kern, f32[2,64,128]{2,1,0:T(8,128)S(1)} %get-tuple-element.20.goal, ...), custom_call_target="tpu_custom_call" | custom-call | tf_op jit(solution)/shard_map/pallas_call | solution.py:260
  17.7 0.1 collective-permute-start.7
  17.8 2.1 %collective-permute-start.6 = (bf16[64,128]{1,0:T(8,128)(2,1)S(1)}, bf16[64,128]{1,0:T(8,128)(2,1)S(1)}, u32[]{:S(2)}, u32[]{:S(2)}) collective-permute-start(bf16[64,128]{1,0:T(8,128)(2,1)S(1)} %get-tuple-element.30), channel_id=1, source_target_pairs={{0,8},{1,9},{4,12},{5,13},{8,0},{9,1},{12,4},{13,5},{2,10},{3,11},... | collective-permute-start | bytes 49160 | tf_op jit(solution)/shard_map/ppermute | solution.py:293
  19.9 1.7 %collective-permute-start.5 = (bf16[64,128]{1,0:T(8,128)(2,1)S(1)}, bf16[64,128]{1,0:T(8,128)(2,1)S(1)}, u32[]{:S(2)}, u32[]{:S(2)}) collective-permute-start(bf16[64,128]{1,0:T(8,128)(2,1)S(1)} %get-tuple-element.31), channel_id=1, source_target_pairs={{0,5},{1,4},{4,1},{5,0},{8,13},{9,12},{12,9},{13,8},{2,7},{3,6},{6... | collective-permute-start | bytes 49160 | tf_op jit(solution)/shard_map/ppermute | solution.py:293
  21.6 0.4 %shard_map.63 = f32[4,64,128]{2,1,0:T(8,128)S(1)} custom-call(bf16[2,2,2,4,64,128]{5,4,3,2,1,0:T(8,128)(2,1)S(1)} %get-tuple-element.14.field, s32[4,8,128]{2,1,0:T(8,128)S(1)} %get-tuple-element.15.counts, bf16[2,4,128,256]{3,2,1,0:T(8,128)(2,1)S(1)} %get-tuple-element.17.both_kern, bf16[2,256,256]{2,1,0:T(8,128)(2,1)S(1)} %get-tuple-element.23.near), custom_call_target="tpu_custom_call" | custom-call | tf_op jit(solution)/shard_map/pallas_call | solution.py:260
  22.0 0.7 %collective-permute-done.7 = bf16[64,128]{1,0:T(8,128)(2,1)S(1)} collective-permute-done((bf16[64,128]{1,0:T(8,128)(2,1)S(1)}, bf16[64,128]{1,0:T(8,128)(2,1)S(1)}, u32[]{:S(2)}, u32[]{:S(2)}) %collective-permute-start.7) | collective-permute-done | bytes 16416 | tf_op jit(solution)/shard_map/ppermute | solution.py:293
  22.8 0.1 collective-permute-done.6
  22.8 0.2 collective-permute-done.5
  23.1 0.6 %collective-permute-start.8 = (bf16[4,64,128]{2,1,0:T(8,128)(2,1)S(1)}, bf16[4,64,128]{2,1,0:T(8,128)(2,1)S(1)}, u32[]{:S(2)}, u32[]{:S(2)}) collective-permute-start(bf16[4,64,128]{2,1,0:T(8,128)(2,1)S(1)} %bitcast_convert_fusion), channel_id=1, source_target_pairs={{0,1},{1,0},{2,3},{3,2},{4,5},{5,4},{6,7},{7,6},{8,9},{9,8},{10,11... | collective-permute-start | bytes 196616 | tf_op jit(solution)/shard_map/ppermute | solution.py:396
  23.7 0.7 %copy.6 = f32[2,64,64]{2,1,0:T(8,128)} copy(f32[2,64,64]{1,2,0:T(8,128)S(1)} %slice_bitcast_fusion) | data formatting | bytes 65536
  24.5 0.2 collective-permute-done.8
  24.6 0.7 %fusion.2 = f32[4,64,128]{2,1,0:T(8,128)} fusion(f32[1,2,2,64,128]{4,3,2,1,0:T(8,128)S(1)} %fusion.1, bf16[4,64,128]{2,1,0:T(8,128)(2,1)S(1)} %collective-permute-done.8), kind=kLoop, calls=%fused_computation.6 | loop fusion | flops 98304 | bytes 327680 | tf_op jit(solution)/shard_map/mul | solution.py:397
  (7 shorter events, 0.1 us)
Async XLA Ops:
  2.3 5.5 %collective-permute-start.1 = (bf16[2,128,128]{2,1,0:T(8,128)(2,1)S(1)}, bf16[2,128,128]{2,1,0:T(8,128)(2,1)S(1)}, u32[]{:S(2)}, u32[]{:S(2)}) collective-permute-start(bf16[2,128,128]{2,1,0:T(8,128)(2,1)S(1)} %get-tuple-element.22), channel_id=1, source_target_pairs={{0,2},{2,0},{1,3},{3,1},{4,6},{6,4},{5,7},{7,5},{8,10},{10,8},{9,1... | collective-permute-start | bytes 196616 | tf_op jit(solution)/shard_map/ppermute | solution.py:275
  5.8 6.7 %copy-start = (f32[2,64,64]{2,1,0:T(8,128)S(1)}, f32[2,64,64]{2,1,0:T(8,128)}, u32[]{:S(2)}) copy-start(f32[2,64,64]{2,1,0:T(8,128)} %target.1) | copy-start | bytes 98308
  5.8 11.2 %collective-permute-start = (bf16[2,4,128,128]{3,2,1,0:T(8,128)(2,1)S(1)}, bf16[2,4,128,128]{3,2,1,0:T(8,128)(2,1)S(1)}, u32[]{:S(2)}, u32[]{:S(2)}) collective-permute-start(bf16[2,4,128,128]{3,2,1,0:T(8,128)(2,1)S(1)} %shard_map.61), channel_id=1, source_target_pairs={{0,2},{2,0},{1,3},{3,1},{4,6},{6,4},{5,7},{7,5},{8,10},{10,8},{9,1... | collective-permute-start | bytes 786440 | tf_op jit(solution)/shard_map/ppermute | solution.py:275
  7.8 6.4 %collective-permute-start.2 = (bf16[2,128,128]{2,1,0:T(8,128)(2,1)S(1)}, bf16[2,128,128]{2,1,0:T(8,128)(2,1)S(1)}, u32[]{:S(2)}, u32[]{:S(2)}) collective-permute-start(bf16[2,128,128]{2,1,0:T(8,128)(2,1)S(1)} %add_convert_fusion.refs_5_), channel_id=1, source_target_pairs={{0,12},{4,8},{8,4},{12,0},{1,13},{5,9},{9,5},{13,1},{2,14},{6,10},... | collective-permute-start | bytes 196616 | tf_op jit(solution)/shard_map/ppermute | solution.py:275
  11.8 5.2 %collective-permute-start.3 = (bf16[2,128,128]{2,1,0:T(8,128)(2,1)S(1)}, bf16[2,128,128]{2,1,0:T(8,128)(2,1)S(1)}, u32[]{:S(2)}, u32[]{:S(2)}) collective-permute-start(bf16[2,128,128]{2,1,0:T(8,128)(2,1)S(1)} %add_convert_fusion.refs_5_), channel_id=1, source_target_pairs={{0,8},{4,12},{8,0},{12,4},{1,9},{5,13},{9,1},{13,5},{2,10},{6,14},... | collective-permute-start | bytes 196616 | tf_op jit(solution)/shard_map/ppermute | solution.py:275
  11.8 5.2 %collective-permute-start.4 = (bf16[2,128,128]{2,1,0:T(8,128)(2,1)S(1)}, bf16[2,128,128]{2,1,0:T(8,128)(2,1)S(1)}, u32[]{:S(2)}, u32[]{:S(2)}) collective-permute-start(bf16[2,128,128]{2,1,0:T(8,128)(2,1)S(1)} %add_convert_fusion.refs_5_), channel_id=1, source_target_pairs={{0,4},{4,0},{8,12},{12,8},{1,5},{5,1},{9,13},{13,9},{2,6},{6,2},{1... | collective-permute-start | bytes 196616 | tf_op jit(solution)/shard_map/ppermute | solution.py:275
  17.7 5.0 %collective-permute-start.7 = (bf16[64,128]{1,0:T(8,128)(2,1)S(1)}, bf16[64,128]{1,0:T(8,128)(2,1)S(1)}, u32[]{:S(2)}, u32[]{:S(2)}) collective-permute-start(bf16[64,128]{1,0:T(8,128)(2,1)S(1)} %get-tuple-element.29), channel_id=1, source_target_pairs={{0,13},{1,12},{4,9},{5,8},{8,5},{9,4},{12,1},{13,0},{2,15},{3,14},... | collective-permute-start | bytes 49160 | tf_op jit(solution)/shard_map/ppermute | solution.py:293
  17.8 5.0 %collective-permute-start.6 = (bf16[64,128]{1,0:T(8,128)(2,1)S(1)}, bf16[64,128]{1,0:T(8,128)(2,1)S(1)}, u32[]{:S(2)}, u32[]{:S(2)}) collective-permute-start(bf16[64,128]{1,0:T(8,128)(2,1)S(1)} %get-tuple-element.30), channel_id=1, source_target_pairs={{0,8},{1,9},{4,12},{5,13},{8,0},{9,1},{12,4},{13,5},{2,10},{3,11},... | collective-permute-start | bytes 49160 | tf_op jit(solution)/shard_map/ppermute | solution.py:293
  19.9 3.2 %collective-permute-start.5 = (bf16[64,128]{1,0:T(8,128)(2,1)S(1)}, bf16[64,128]{1,0:T(8,128)(2,1)S(1)}, u32[]{:S(2)}, u32[]{:S(2)}) collective-permute-start(bf16[64,128]{1,0:T(8,128)(2,1)S(1)} %get-tuple-element.31), channel_id=1, source_target_pairs={{0,5},{1,4},{4,1},{5,0},{8,13},{9,12},{12,9},{13,8},{2,7},{3,6},{6... | collective-permute-start | bytes 49160 | tf_op jit(solution)/shard_map/ppermute | solution.py:293
  23.1 1.5 %collective-permute-start.8 = (bf16[4,64,128]{2,1,0:T(8,128)(2,1)S(1)}, bf16[4,64,128]{2,1,0:T(8,128)(2,1)S(1)}, u32[]{:S(2)}, u32[]{:S(2)}) collective-permute-start(bf16[4,64,128]{2,1,0:T(8,128)(2,1)S(1)} %bitcast_convert_fusion), channel_id=1, source_target_pairs={{0,1},{1,0},{2,3},{3,2},{4,5},{5,4},{6,7},{7,6},{8,9},{9,8},{10,11... | collective-permute-start | bytes 196616 | tf_op jit(solution)/shard_map/ppermute | solution.py:396
